TPU v7x, 32 devices: a whole 2x2x4 slice. The times are simulated.
32 devices in a mesh: dp: 8 (over y, x, core), tensor: 4 (over z).
Axes of the slice: x: 2, y: 2, z: 4, core: 2. Of those that a mesh axis runs over, the one named last changes fastest.
Arguments:
- tokens: bfloat16 [4096, 768], P(('dp', 'tensor')), may hold values from -2.5 to 2.5
- condition: bfloat16 [8, 768], P('dp'), may hold values from -2.5 to 2.5
- modulate_weight: bfloat16 [768, 4608], P(None, 'tensor'), may hold values from -0.21875 to 0.21875
- modulate_bias: float32 [4608], P('tensor'), may hold values from -0.75 to 0.75
- heads_weight: bfloat16 [3, 768, 768], P(None, None, 'tensor'), may hold values from -0.21875 to 0.21875
- heads_bias: float32 [2, 768], P(None, 'tensor'), may hold values from -0.75 to 0.75
- output_weight: bfloat16 [768, 768], P('tensor'), may hold values from -0.875 to 0.875
- output_bias: float32 [768], replicated, may hold values from -0.75 to 0.75
- first_weight: bfloat16 [768, 3072], P(None, 'tensor'), may hold values from -0.21875 to 0.21875
- first_bias: float32 [3072], P('tensor'), may hold values from -0.75 to 0.75
- second_weight: bfloat16 [3072, 768], P('tensor'), may hold values from -0.109375 to 0.109375
- second_bias: float32 [768], replicated, may hold values from -0.75 to 0.75
- cotangent: bfloat16 [4096, 768], P(('dp', 'tensor')), may hold values from -2.5 to 2.5
Outputs:
- output: bfloat16 [4096, 768], P(('dp', 'tensor'))
- token_grad: float32 [4096, 768], P(('dp', 'tensor'))
- modulate_weight_grad: float32 [768, 4608], P('dp', 'tensor')
- modulate_bias_grad: float32 [4608], P('tensor')
- heads_weight_grad: float32 [3, 768, 768], P(None, 'dp', 'tensor')
- heads_bias_grad: float32 [2, 768], P(None, 'tensor')
- output_weight_grad: float32 [768, 768], P('tensor', 'dp')
- output_bias_grad: float32 [768], replicated
- first_weight_grad: float32 [768, 3072], P('dp', 'tensor')
- first_bias_grad: float32 [3072], P('tensor')
- second_weight_grad: float32 [3072, 768], P('tensor', 'dp')
- second_bias_grad: float32 [768], replicated
All inputs are finite; a program needn't handle non-finite values.
Results may differ from a plain program's by a relative error of at most 0.012.
The roundings to bfloat16 on the way count: a program that leaves them out, or rounds other values in their place, can miss the bound.
Values may be sent and summed in bfloat16 or wider, within the bound.
A program may use at most 128 MiB of HBM per device.

v0:
```python
from functools import partial

import jax
import jax.numpy as jnp
from jax import lax
from jax.sharding import PartitionSpec as P

HD = 64
LEN = 512


EPSILON = 1e-06
HIGHEST_PRECISION = lax.Precision.HIGHEST


def layer_norm(values):
    centred = values - jnp.mean(values, axis=-1, keepdims=True)
    inverse = lax.rsqrt(jnp.mean(centred * centred, axis=-1, keepdims=True) + EPSILON)
    return (centred * inverse, inverse)


def norm_back(grade, normed, inverse):
    return inverse * (
        grade
        - jnp.mean(grade, axis=-1, keepdims=True)
        - normed * jnp.mean(grade * normed, axis=-1, keepdims=True)
    )


def matmul(left, right):
    return jnp.dot(left, right, preferred_element_type=jnp.float32)


def left_contract(left, right):
    return lax.dot_general(
        left, right, (((0,), (0,)), ((), ())), preferred_element_type=jnp.float32
    )


def right_contract(left, right):
    return lax.dot_general(
        left, right, (((1,), (1,)), ((), ())), preferred_element_type=jnp.float32
    )


def exact_left(left, right):
    return lax.dot_general(
        left,
        right,
        (((0,), (0,)), ((), ())),
        precision=HIGHEST_PRECISION,
        preferred_element_type=jnp.float32,
    )


def head_cols(values, head):
    return values[:, head * HD : (head + 1) * HD]


def attend_forward(blocks):
    query_block, key_block, value_block = blocks
    outputs = []
    sums = []
    for head in range(query_block.shape[1] // HD):
        scores = right_contract(head_cols(query_block, head), head_cols(key_block, head)) * HD ** (
            -0.5
        )
        peak = jnp.max(scores, axis=-1, keepdims=True)
        expo = jnp.exp(scores - peak)
        total = jnp.sum(expo, axis=-1, keepdims=True)
        probability = (expo / total).astype(jnp.bfloat16)
        outputs.append(matmul(probability, head_cols(value_block, head)))
        sums.append((peak + jnp.log(total))[:, 0])
    return (jnp.concatenate(outputs, axis=1).astype(jnp.bfloat16), jnp.stack(sums))


def attend_backward(blocks):
    query_block, key_block, value_block, grade_block, logsum = blocks
    query_parts = []
    key_parts = []
    value_parts = []
    for head in range(query_block.shape[1] // HD):
        query_head = head_cols(query_block, head)
        key_head = head_cols(key_block, head)
        grade_head = head_cols(grade_block, head)
        scores = right_contract(query_head, key_head) * HD ** (-0.5)
        probability = jnp.exp(scores - logsum[head][:, None])
        value_parts.append(left_contract(probability.astype(jnp.bfloat16), grade_head))
        prob_grad = right_contract(grade_head, head_cols(value_block, head))
        score_grad = probability * (
            prob_grad - jnp.sum(probability * prob_grad, axis=-1, keepdims=True)
        )
        score_low = score_grad.astype(jnp.bfloat16)
        query_parts.append(matmul(score_low, key_head) * HD ** (-0.5))
        key_parts.append(left_contract(score_low, query_head) * HD ** (-0.5))
    return jnp.stack(
        [
            jnp.concatenate(query_parts, axis=1),
            jnp.concatenate(key_parts, axis=1),
            jnp.concatenate(value_parts, axis=1),
        ]
    ).astype(jnp.bfloat16)


def local(
    tokens,
    condition,
    modulate_weight,
    modulate_bias,
    heads_weight,
    heads_bias,
    output_weight,
    output_bias,
    first_weight,
    first_bias,
    second_weight,
    second_bias,
    cotangent,
):
    tensor_rank = lax.axis_index("tensor")
    row_count = tokens.shape[0]
    model_width = tokens.shape[1]
    latent_count = condition.shape[0]
    local_width = heads_weight.shape[2]
    group_rows = latent_count * LEN
    silu_cond = jax.nn.silu(condition.astype(jnp.float32)).astype(jnp.bfloat16)
    modulate_local = matmul(silu_cond, modulate_weight) + modulate_bias
    modulation = lax.all_gather(modulate_local, "tensor", axis=1, tiled=True)
    latent_of_row = (tensor_rank * row_count + jnp.arange(row_count, dtype=jnp.int32)) // LEN
    selector = (
        latent_of_row[:, None] == jnp.arange(latent_count, dtype=jnp.int32)[None, :]
    ).astype(jnp.float32)
    row_mods = jnp.dot(selector, modulation, precision=HIGHEST_PRECISION)
    pieces = [row_mods[:, member * model_width : (member + 1) * model_width] for member in range(6)]
    shift_attn, scale_attn, gate_attn, shift_feed, scale_feed, gate_feed = pieces
    residual = tokens.astype(jnp.float32)
    normed_first, inverse_first = layer_norm(residual)
    attention_in = (normed_first * (1.0 + scale_attn) + shift_attn).astype(jnp.bfloat16)
    attention_all = lax.all_gather(attention_in, "tensor", axis=0, tiled=True)
    projected = jnp.einsum(
        "td,sde->ste", attention_all, heads_weight, preferred_element_type=jnp.float32
    )
    query_rows = (projected[0] + heads_bias[0]).astype(jnp.bfloat16)
    key_rows = projected[1].astype(jnp.bfloat16)
    value_rows = (projected[2] + heads_bias[1]).astype(jnp.bfloat16)
    shaped = (latent_count, LEN, local_width)
    query_blocks = query_rows.reshape(shaped)
    key_blocks = key_rows.reshape(shaped)
    value_blocks = value_rows.reshape(shaped)
    mixture, logsum = lax.map(attend_forward, (query_blocks, key_blocks, value_blocks))
    mixture = mixture.reshape(group_rows, local_width)
    branch_attn = (
        lax.psum_scatter(
            matmul(
                lax.slice_in_dim(mixture, 0, lax.axis_size("tensor") * row_count, axis=0),
                output_weight,
            ),
            "tensor",
            scatter_dimension=0,
            tiled=True,
        )
        + output_bias
    )
    residual_mid = residual + gate_attn * branch_attn
    normed_second, inverse_second = layer_norm(residual_mid)
    feed_in = (normed_second * (1.0 + scale_feed) + shift_feed).astype(jnp.bfloat16)
    feed_all = lax.all_gather(feed_in, "tensor", axis=0, tiled=True)
    hidden_pre = matmul(feed_all, first_weight) + first_bias
    activated = jax.nn.gelu(hidden_pre, approximate=True).astype(jnp.bfloat16)
    branch_feed = (
        lax.psum_scatter(
            matmul(
                lax.slice_in_dim(activated, 0, lax.axis_size("tensor") * row_count, axis=0),
                second_weight,
            ).astype(jnp.bfloat16),
            "tensor",
            scatter_dimension=0,
            tiled=True,
        ).astype(jnp.float32)
        + second_bias
    )
    output = (residual_mid + gate_feed * branch_feed).astype(jnp.bfloat16)
    tangent = cotangent.astype(jnp.float32)
    feed_grad = (gate_feed * tangent).astype(jnp.bfloat16)
    feed_grad_all = lax.all_gather(feed_grad, "tensor", axis=0, tiled=True)
    grad_second_bias = jnp.sum(feed_grad_all, axis=0, dtype=jnp.float32)
    grad_second_weight = left_contract(activated, feed_grad_all)
    activated_grad = right_contract(feed_grad_all, second_weight)
    unused_value, gelu_back = jax.vjp(partial(jax.nn.gelu, approximate=True), hidden_pre)
    pre_grad = gelu_back(activated_grad)[0].astype(jnp.bfloat16)
    grad_first_bias = jnp.sum(pre_grad, axis=0, dtype=jnp.float32)
    grad_first_weight = left_contract(feed_all, pre_grad)
    feed_in_grad = lax.psum_scatter(
        right_contract(
            lax.slice_in_dim(pre_grad, 0, lax.axis_size("tensor") * row_count, axis=0), first_weight
        ),
        "tensor",
        scatter_dimension=0,
        tiled=True,
    )
    mid_grad = tangent + norm_back(feed_in_grad * (1.0 + scale_feed), normed_second, inverse_second)
    attn_grad = (gate_attn * mid_grad).astype(jnp.bfloat16)
    attn_grad_all = lax.all_gather(attn_grad, "tensor", axis=0, tiled=True)
    grad_output_bias = jnp.sum(attn_grad_all, axis=0, dtype=jnp.float32)
    grad_output_weight = left_contract(mixture, attn_grad_all)
    mixture_grad = right_contract(attn_grad_all, output_weight).astype(jnp.bfloat16)
    stacked_grads = lax.map(
        attend_backward,
        (query_blocks, key_blocks, value_blocks, mixture_grad.reshape(shaped), logsum),
    )
    heads_grad = jnp.swapaxes(stacked_grads, 0, 1).reshape(3, group_rows, local_width)
    grad_heads_weight = jnp.einsum(
        "td,ste->sde", attention_all, heads_grad, preferred_element_type=jnp.float32
    )
    grad_heads_bias = jnp.stack(
        [
            jnp.sum(heads_grad[0], axis=0, dtype=jnp.float32),
            jnp.sum(heads_grad[2], axis=0, dtype=jnp.float32),
        ]
    )
    attn_in_grad = lax.psum_scatter(
        jnp.einsum("ste,sde->td", heads_grad, heads_weight, preferred_element_type=jnp.float32),
        "tensor",
        scatter_dimension=0,
        tiled=True,
    )
    token_grad = mid_grad + norm_back(
        attn_in_grad * (1.0 + scale_attn), normed_first, inverse_first
    )
    row_terms = jnp.concatenate(
        [
            attn_in_grad,
            attn_in_grad * normed_first,
            mid_grad * branch_attn,
            feed_in_grad,
            feed_in_grad * normed_second,
            tangent * branch_feed,
        ],
        axis=1,
    )
    modulation_partial = exact_left(selector, row_terms)
    modulation_grad = lax.psum_scatter(
        modulation_partial, "tensor", scatter_dimension=1, tiled=True
    )
    grad_modulate_bias = jnp.sum(modulation_grad, axis=0)
    bias_total = lax.psum(
        (grad_modulate_bias, grad_heads_bias, grad_output_bias, grad_first_bias, grad_second_bias),
        "dp",
    )
    cond_all, modulation_all = (
        lax.all_gather(silu_cond.astype(jnp.float32), "dp", axis=0, tiled=True),
        lax.all_gather(modulation_grad, "dp", axis=0, tiled=True),
    )
    share = model_width // lax.axis_size("dp")
    cond_share = lax.dynamic_slice_in_dim(cond_all, lax.axis_index("dp") * share, share, 1)
    grad_modulate_weight = exact_left(cond_share, modulation_all)
    matrices = (
        lax.psum_scatter(grad_heads_weight, "dp", scatter_dimension=1, tiled=True),
        lax.psum_scatter(grad_output_weight, "dp", scatter_dimension=1, tiled=True),
        lax.psum_scatter(grad_first_weight, "dp", scatter_dimension=0, tiled=True),
        lax.psum_scatter(grad_second_weight, "dp", scatter_dimension=1, tiled=True),
    )
    return (
        output,
        token_grad,
        grad_modulate_weight,
        bias_total[0],
        matrices[0],
        bias_total[1],
        matrices[1],
        bias_total[2],
        matrices[2],
        bias_total[3],
        matrices[3],
        bias_total[4],
    )


def solution(mesh):
    in_specs = (
        P(("dp", "tensor"), None),
        P("dp", None),
        P(None, "tensor"),
        P("tensor"),
        P(None, None, "tensor"),
        P(None, "tensor"),
        P("tensor", None),
        P(),
        P(None, "tensor"),
        P("tensor"),
        P("tensor", None),
        P(),
        P(("dp", "tensor"), None),
    )
    out_specs = (
        P(("dp", "tensor"), None),
        P(("dp", "tensor"), None),
        P("dp", "tensor"),
        P("tensor"),
        P(None, "dp", "tensor"),
        P(None, "tensor"),
        P("tensor", "dp"),
        P(),
        P("dp", "tensor"),
        P("tensor"),
        P("tensor", "dp"),
        P(),
    )
    return jax.shard_map(local, mesh=mesh, in_specs=in_specs, out_specs=out_specs, check_vma=False)
```

profile of v0, /device:TPU:0, one launch (start us, length us, event | category | flops | bytes accessed | tf_op | source)
XLA Modules:
  0.0 488.1 jit_solution(5927712620343426322)
XLA Ops:
  11.4 14.9 %all-gather.1 = f32[4,1,1152]{2,1,0:T(1,128)S(1)} all-gather(f32[1,1,1152]{2,1,0:T(1,128)S(1)} %reshape.153), channel_id=2, replica_groups=mesh['dp'=8,'tensor'=4] {'tensor'}, dimensions={0}, use_global_device_ids=true | all-gather | bytes 23040 | tf_op jit(solution)/shard_map/all_gather | solution.py:128
  27.0 17.7 %all_gather.22 = bf16[512,768]{1,0:T(8,128)(2,1)S(1)} all-gather(bf16[128,768]{1,0:T(8,128)(2,1)S(1)} %fusion.33), channel_id=1, replica_groups=mesh['dp'=8,'tensor'=4] {'tensor'}, dimensions={0}, use_global_device_ids=true | all-gather | bytes 983040 | tf_op jit(solution)/shard_map/all_gather | solution.py:139
  49.6 1.6 fusion.50
  51.3 35.5 %reduce-scatter.16.cloned.1.call-done = f32[128,768]{1,0:T(8,128)} async-done(((f32[512,768]{1,0:T(8,128)}), f32[128,768]{1,0:T(8,128)}) %reduce-scatter.16.cloned.1.call-update) | async-done | bytes 393232 | tf_op jit(solution)/shard_map/reduce_scatter | solution.py:153
  88.3 1.6 fusion.40
  89.9 18.1 %all_gather.24 = bf16[512,768]{1,0:T(8,128)(2,1)S(1)} all-gather(bf16[128,768]{1,0:T(8,128)(2,1)S(1)} %get-tuple-element.91), channel_id=1, replica_groups=mesh['dp'=8,'tensor'=4] {'tensor'}, dimensions={0}, use_global_device_ids=true | all-gather | bytes 983040 | tf_op jit(solution)/shard_map/all_gather | solution.py:185
  108.0 17.5 %all_gather.23 = bf16[512,768]{1,0:T(8,128)(2,1)S(1)} all-gather(bf16[128,768]{1,0:T(8,128)(2,1)S(1)} %get-tuple-element.92), channel_id=1, replica_groups=mesh['dp'=8,'tensor'=4] {'tensor'}, dimensions={0}, use_global_device_ids=true | all-gather | bytes 983040 | tf_op jit(solution)/shard_map/all_gather | solution.py:167
  127.1 3.4 convert_reduce_fusion.1
  131.4 2.0 fusion.106
  133.5 3.8 convolution_convert_fusion
  138.7 29.7 %reduce-scatter.20.cloned.1.call-done = f32[128,768]{1,0:T(8,128)} async-done(((f32[512,768]{1,0:T(8,128)}), f32[128,768]{1,0:T(8,128)}) %reduce-scatter.20.cloned.1.call-update) | async-done | bytes 393232 | tf_op jit(solution)/shard_map/reduce_scatter | solution.py:193
  170.3 22.8 %reduce-scatter.18.cloned.1.call-done = bf16[128,768]{1,0:T(8,128)(2,1)} async-done(((bf16[512,768]{1,0:T(8,128)(2,1)}), bf16[128,768]{1,0:T(8,128)(2,1)}) %reduce-scatter.18.cloned.1.call-update) | async-done | bytes 196624 | tf_op jit(solution)/shard_map/reduce_scatter | solution.py:171
  193.1 2.5 multiply_convert_fusion.4
  195.7 18.3 %all_gather.25 = bf16[512,768]{1,0:T(8,128)(2,1)S(1)} all-gather(bf16[128,768]{1,0:T(8,128)(2,1)S(1)} %get-tuple-element.86), channel_id=1, replica_groups=mesh['dp'=8,'tensor'=4] {'tensor'}, dimensions={0}, use_global_device_ids=true | all-gather | bytes 983040 | tf_op jit(solution)/shard_map/all_gather | solution.py:203
  220.9 2.0 convolution_bitcast_fusion.2
  225.6 3.2 convolution_bitcast_fusion.1
  228.8 4.2 copy.29
  233.0 4.7 reshape.172
  237.8 19.9 %reduce-scatter.22.cloned.1.call-done = f32[128,768]{1,0:T(8,128)} async-done(((f32[512,768]{1,0:T(8,128)}), f32[128,768]{1,0:T(8,128)}) %reduce-scatter.22.cloned.1.call-update) | async-done | bytes 393232 | tf_op jit(solution)/shard_map/reduce_scatter | solution.py:221
  259.1 2.0 fusion.38
  262.2 3.5 convolution_bitcast_fusion
  265.8 4.2 fusion.97
  270.1 3.6 fusion.107
  274.3 9.2 %all-gather.2 = f32[8,1,768]{2,1,0:T(1,128)S(1)} all-gather(f32[1,1,768]{2,1,0:T(1,128)S(1)} %bitcast_convert_fusion), channel_id=1, replica_groups=mesh['dp'=8,'tensor'=4] {'dp'}, dimensions={0}, use_global_device_ids=true | all-gather | bytes 27648 | tf_op jit(solution)/shard_map/all_gather | solution.py:251
  285.4 9.2 %reduce-scatter.32.cloned.1.call-done = f32[96,192]{1,0:T(8,128)} async-done(((f32[768,192]{1,0:T(8,128)}), f32[96,192]{1,0:T(8,128)}) %reduce-scatter.32.cloned.1.call-update) | async-done | bytes 73744
  294.6 1.6 copy.32
  296.3 42.0 %reduce-scatter.30.cloned.1.call-done = f32[96,576]{1,0:T(8,128)} async-done(((f32[768,576]{1,0:T(8,128)}), f32[96,576]{1,0:T(8,128)}) %reduce-scatter.30.cloned.1.call-update) | async-done | bytes 221200
  340.1 48.6 %reduce-scatter.28.cloned.1.call-done = f32[1152,1]{1,0:T(8,128)} async-done(((f32[4608,1]{1,0:T(8,128)}), f32[1152,1]{1,0:T(8,128)}) %reduce-scatter.28.cloned.1.call-update) | async-done | bytes 4624
  391.3 24.4 %all-reduce = (f32[1152]{0:T(1024)}, f32[2,192]{1,0:T(2,128)}, f32[768]{0:T(1024)}, f32[768]{0:T(1024)}, f32[768]{0:T(1024)}) all-reduce(f32[1152]{0:T(1024)S(1)} %bitcast_reduce_fusion, f32[2,192]{1,0:T(2,128)S(1)} %pad_maximum_fusion.6, f32[768]{0:T(1024)S(1)} %convert_reduce_fusion.2, ...), channel_id=1, replica_groups=mesh['dp'=8,'tensor'=4] {'dp'}, use_global_device_ids=true, to_apply=%region_22.23 | all-reduce | flops 3840 | bytes 30720 | tf_op jit(solution)/shard_map/psum | solution.py:246
  415.7 8.1 %all-gather.3 = f32[8,1,1152]{2,1,0:T(1,128)S(1)} all-gather(f32[1,1,1152]{2,1,0:T(1,128)S(1)} %bitcast.98), channel_id=1, replica_groups=mesh['dp'=8,'tensor'=4] {'dp'}, dimensions={0}, use_global_device_ids=true | all-gather | bytes 41472 | tf_op jit(solution)/shard_map/all_gather | solution.py:252
  425.2 10.0 %reduce-scatter.26.cloned.1.call-done = f32[768,96]{0,1:T(8,128)} async-done(((f32[768,768]{0,1:T(8,128)}), f32[768,96]{0,1:T(8,128)}) %reduce-scatter.26.cloned.1.call-update) | async-done | bytes 294928 | tf_op jit(solution)/shard_map/reduce_scatter | solution.py:261
  435.1 46.5 %reduce-scatter.24.cloned.1.call-done = f32[96,768]{1,0:T(8,128)} async-done(((f32[768,768]{1,0:T(8,128)}), f32[96,768]{1,0:T(8,128)}) %reduce-scatter.24.cloned.1.call-update) | async-done | bytes 294928 | tf_op jit(solution)/shard_map/reduce_scatter | solution.py:260
  (226 shorter events, 37.0 us)
Async XLA Ops:
  7.2 79.6 %reduce-scatter.16.cloned.1.call-start = ((), (), s32[]{:S(2)}) async-start(), calls=%async_computation.9 | async-start | bytes 1966080 | tf_op jit(solution)/shard_map/reduce_scatter | solution.py:153
  8.4 18.3 %copy-start.52 = (f32[128]{0:T(128)}, f32[128]{0:T(128)S(1)}, u32[]{:S(2)}) copy-start(f32[128]{0:T(128)S(1)} %broadcast_multiply_fusion.6) | copy-start | bytes 1540
  9.6 17.2 %copy-start.61 = (f32[128]{0:T(128)}, f32[128]{0:T(128)S(1)}, u32[]{:S(2)}) copy-start(f32[128]{0:T(128)S(1)} %add_rsqrt_fusion.1) | copy-start | bytes 1540
  11.4 15.4 %copy-start.8 = (bf16[128,768]{1,0:T(8,128)(2,1)S(1)}, bf16[128,768]{1,0:T(8,128)(2,1)}, u32[]{:S(2)}) copy-start(bf16[128,768]{1,0:T(8,128)(2,1)} %param.13) | copy-start | bytes 589828
  26.8 18.6 %copy-start.5 = (f32[128,4608]{1,0:T(8,128)}, f32[128,4608]{1,0:T(8,128)S(1)}, u32[]{:S(2)}) copy-start(f32[128,4608]{1,0:T(8,128)S(1)} %broadcast_multiply_fusion) | copy-start | bytes 7077892
  26.8 18.0 %copy-start.23 = (bf16[3,768,192]{1,2,0:T(8,128)(2,1)S(1)}, bf16[3,768,192]{1,2,0:T(8,128)(2,1)}, u32[]{:S(2)}) copy-start(bf16[3,768,192]{1,2,0:T(8,128)(2,1)} %param.17) | copy-start | bytes 2654212
  49.6 37.1 %copy-start.46 = (f32[768]{0:T(1024)S(1)}, f32[768]{0:T(1024)}, u32[]{:S(2)}) copy-start(f32[768]{0:T(1024)} %param.20) | copy-start | bytes 9220
  51.2 117.2 %reduce-scatter.20.cloned.1.call-start = ((), (), s32[]{:S(2)}) async-start(), calls=%async_computation.11 | async-start | bytes 1966080 | tf_op jit(solution)/shard_map/reduce_scatter | solution.py:193
  88.0 20.0 %copy-start.49 = (f32[128]{0:T(128)}, f32[128]{0:T(128)S(1)}, u32[]{:S(2)}) copy-start(f32[128]{0:T(128)S(1)} %broadcast_multiply_fusion.5) | copy-start | bytes 1540
  88.2 19.8 %copy-start.59 = (f32[128]{0:T(128)}, f32[128]{0:T(128)S(1)}, u32[]{:S(2)}) copy-start(f32[128]{0:T(128)S(1)} %add_rsqrt_fusion) | copy-start | bytes 1540
  88.3 37.3 %copy-start.65 = (bf16[768,768]{1,0:T(8,128)(2,1)S(1)}, bf16[768,768]{1,0:T(8,128)(2,1)}, u32[]{:S(2)}) copy-start(bf16[768,768]{1,0:T(8,128)(2,1)} %param.23) | copy-start | bytes 3538948
  108.0 17.5 %copy-start.12 = (bf16[512,768]{1,0:T(8,128)(2,1)}, bf16[512,768]{1,0:T(8,128)(2,1)S(1)}, u32[]{:S(2)}) copy-start(bf16[512,768]{1,0:T(8,128)(2,1)S(1)} %all_gather.24) | copy-start | bytes 2359300
  133.4 59.7 %reduce-scatter.18.cloned.1.call-start = ((), (), s32[]{:S(2)}) async-start(), calls=%async_computation.10 | async-start | bytes 983040 | tf_op jit(solution)/shard_map/reduce_scatter | solution.py:171
  137.3 120.4 %reduce-scatter.22.cloned.1.call-start = ((), (), s32[]{:S(2)}) async-start(), calls=%async_computation.12 | async-start | bytes 1966080 | tf_op jit(solution)/shard_map/reduce_scatter | solution.py:221
  193.1 20.8 %copy-start.22 = (bf16[192,768]{1,0:T(8,128)(2,1)S(1)}, bf16[192,768]{1,0:T(8,128)(2,1)}, u32[]{:S(2)}) copy-start(bf16[192,768]{1,0:T(8,128)(2,1)} %param.19) | copy-start | bytes 884740
  195.7 18.7 %copy-start.4 = (f32[512,512]{0,1:T(8,128)S(1)}, f32[512,512]{0,1:T(8,128)}, u32[]{:S(2)}) copy-start(f32[512,512]{0,1:T(8,128)} %copy-done.3) | copy-start | bytes 3145732
  195.7 19.0 %copy-start.26 = (bf16[512,192]{0,1:T(8,128)(2,1)S(1)}, bf16[512,192]{0,1:T(8,128)(2,1)}, u32[]{:S(2)}) copy-start(bf16[512,192]{0,1:T(8,128)(2,1)} %copy-done.25) | copy-start | bytes 589828
  223.0 71.7 %reduce-scatter.32.cloned.1.call-start = ((), (), s32[]{:S(2)}) async-start(), calls=%async_computation.17 | async-start | bytes 884736
  225.5 112.7 %reduce-scatter.30.cloned.1.call-start = ((), (), s32[]{:S(2)}) async-start(), calls=%async_computation.16 | async-start | bytes 2211840
  237.7 20.0 %copy-start.53 = (f32[128]{0:T(128)S(1)}, f32[128]{0:T(128)}, u32[]{:S(2)}) copy-start(f32[128]{0:T(128)} %copy-done.52) | copy-start | bytes 1540
  237.7 20.0 %copy-start.62 = (f32[128]{0:T(128)S(1)}, f32[128]{0:T(128)}, u32[]{:S(2)}) copy-start(f32[128]{0:T(128)} %copy-done.61) | copy-start | bytes 1540
  237.7 21.4 %copy-start.11 = (f32[128,768]{1,0:T(8,128)S(1)}, f32[128,768]{1,0:T(8,128)}, u32[]{:S(2)}) copy-start(f32[128,768]{1,0:T(8,128)} %get-tuple-element.87) | copy-start | bytes 1179652
  237.7 23.4 %copy-start.47 = (f32[768]{0:T(1024)S(1)}, f32[768]{0:T(1024)}, u32[]{:S(2)}) copy-start(f32[768]{0:T(1024)} %param.20) | copy-start | bytes 9220
  237.7 151.0 %reduce-scatter.28.cloned.1.call-start = ((), (), s32[]{:S(2)}) async-start(), calls=%async_computation.15 | async-start | bytes 2949120
  265.7 169.4 %reduce-scatter.26.cloned.1.call-start = ((), (), s32[]{:S(2)}) async-start(), calls=%async_computation.14 | async-start | bytes 2654208 | tf_op jit(solution)/shard_map/reduce_scatter | solution.py:261
  270.0 211.6 %reduce-scatter.24.cloned.1.call-start = ((), (), s32[]{:S(2)}) async-start(), calls=%async_computation.13 | async-start | bytes 2654208 | tf_op jit(solution)/shard_map/reduce_scatter | solution.py:260
  273.6 11.3 %copy-start.34 = (bf16[512,64]{0,1:T(8,128)(2,1)S(1)}, bf16[512,64]{0,1:T(8,128)(2,1)}, u32[]{:S(2)}) copy-start(bf16[512,64]{0,1:T(8,128)(2,1)} %copy-done.33) | copy-start | bytes 196612
  273.6 11.3 %copy-start.38 = (bf16[512,64]{0,1:T(8,128)(2,1)S(1)}, bf16[512,64]{0,1:T(8,128)(2,1)}, u32[]{:S(2)}) copy-start(bf16[512,64]{0,1:T(8,128)(2,1)} %copy-done.37) | copy-start | bytes 196612
  273.7 11.4 %copy-start.32 = (bf16[512,64]{0,1:T(8,128)(2,1)S(1)}, bf16[512,64]{0,1:T(8,128)(2,1)}, u32[]{:S(2)}) copy-start(bf16[512,64]{0,1:T(8,128)(2,1)} %copy-done.31) | copy-start | bytes 196612
  273.7 11.4 %copy-start.36 = (bf16[512,64]{0,1:T(8,128)(2,1)S(1)}, bf16[512,64]{0,1:T(8,128)(2,1)}, u32[]{:S(2)}) copy-start(bf16[512,64]{0,1:T(8,128)(2,1)} %copy-done.35) | copy-start | bytes 196612
  273.7 11.4 %copy-start.40 = (bf16[512,64]{0,1:T(8,128)(2,1)S(1)}, bf16[512,64]{0,1:T(8,128)(2,1)}, u32[]{:S(2)}) copy-start(bf16[512,64]{0,1:T(8,128)(2,1)} %copy-done.39) | copy-start | bytes 196612
  285.2 106.0 %copy-start.63 = (f32[768]{0:T(1024)S(1)}, f32[768]{0:T(1024)}, u32[]{:S(2)}) copy-start(f32[768]{0:T(1024)} %get-tuple-element.84) | copy-start | bytes 9220
  (44 other events, 81.1 us)
Sparse Core Ops, SparseCore 0:
  51.3 35.3 reduce-scatter.15
  133.5 34.8 reduce-scatter.19
  170.8 22.3 reduce-scatter.17
  223.1 34.5 reduce-scatter.21
  260.6 33.9 reduce-scatter.31
  297.9 40.2 reduce-scatter.29
  340.6 47.9 reduce-scatter.27
  393.0 42.1 reduce-scatter.25
  439.1 42.4 reduce-scatter.23
where the time goes:
time: 489 us; the launch traced here: 488 us
  waiting for transfers between devices  264 us (54%)
  blocking collectives  128 us (26%)
  matrix products  38.3 us (8%)
  local copies, waits for them, and re-layouts  23.5 us (5%)
  other arithmetic  18.5 us (4%)
  between operations  14.8 us (3%)
    unnamed x12, waiting for transfers between devices  99.9 us
    reduce_scatter x1, waiting for transfers between devices, local(): lax.psum_scatter(grad_first_weight, 'dp', scatter_dimension=0, tiled=True)  46.5 us
    reduce_scatter x1, waiting for transfers between devices, local(): lax.psum_scatter(matmul(lax.slice_in_dim(mixture, 0, lax.axis_size('tenso...  35.5 us
    reduce_scatter x1, waiting for transfers between devices, local(): lax.psum_scatter(right_contract(lax.slice_in_dim(pre_grad, 0, lax.axis_si...  29.7 us
    psum x1, blocking collectives, local(): lax.psum((grad_modulate_bias, grad_heads_bias, grad_output_bias, grad_fir...  24.4 us
    reduce_scatter x1, waiting for transfers between devices, local(): lax.psum_scatter(matmul(lax.slice_in_dim(activated, 0, lax.axis_size('ten...  22.8 us
    unnamed x143, local copies, waits for them, and re-layouts  21.3 us
    reduce_scatter x1, waiting for transfers between devices, local(): lax.psum_scatter(jnp.einsum('ste,sde->td', heads_grad, heads_weight, pref...  19.9 us
  transfers between devices with their start and end apart: 9, of which 9 were waited for; matrix products, arithmetic and copies ran while one was open for 9% of the time, Pallas kernels for 0%

commit v1 on v0

v1 whole, which is shorter than its diff:
```python
from functools import partial

import jax
import jax.numpy as jnp
from jax import lax
from jax.experimental import pallas as pl
from jax.experimental.pallas import tpu as pltpu
from jax.sharding import PartitionSpec as P

HD = 64
LEN = 512


EPSILON = 1e-06
HIGHEST_PRECISION = lax.Precision.HIGHEST


def layer_norm(values):
    centred = values - jnp.mean(values, axis=-1, keepdims=True)
    inverse = lax.rsqrt(jnp.mean(centred * centred, axis=-1, keepdims=True) + EPSILON)
    return (centred * inverse, inverse)


def norm_back(grade, normed, inverse):
    return inverse * (
        grade
        - jnp.mean(grade, axis=-1, keepdims=True)
        - normed * jnp.mean(grade * normed, axis=-1, keepdims=True)
    )


def matmul(left, right):
    return jnp.dot(left, right, preferred_element_type=jnp.float32)


def left_contract(left, right):
    return lax.dot_general(
        left, right, (((0,), (0,)), ((), ())), preferred_element_type=jnp.float32
    )


def right_contract(left, right):
    return lax.dot_general(
        left, right, (((1,), (1,)), ((), ())), preferred_element_type=jnp.float32
    )


def exact_left(left, right):
    return lax.dot_general(
        left,
        right,
        (((0,), (0,)), ((), ())),
        precision=HIGHEST_PRECISION,
        preferred_element_type=jnp.float32,
    )


def head_cols(values, head):
    return values[:, head * HD : (head + 1) * HD]


def attend_forward(blocks):
    query_block, key_block, value_block = blocks
    outputs = []
    sums = []
    for head in range(query_block.shape[1] // HD):
        scores = right_contract(head_cols(query_block, head), head_cols(key_block, head)) * HD ** (
            -0.5
        )
        peak = jnp.max(scores, axis=-1, keepdims=True)
        expo = jnp.exp(scores - peak)
        total = jnp.sum(expo, axis=-1, keepdims=True)
        probability = (expo / total).astype(jnp.bfloat16)
        outputs.append(matmul(probability, head_cols(value_block, head)))
        sums.append((peak + jnp.log(total))[:, 0])
    return (jnp.concatenate(outputs, axis=1).astype(jnp.bfloat16), jnp.stack(sums))


def attend_backward(blocks):
    query_block, key_block, value_block, grade_block, logsum = blocks
    query_parts = []
    key_parts = []
    value_parts = []
    for head in range(query_block.shape[1] // HD):
        query_head = head_cols(query_block, head)
        key_head = head_cols(key_block, head)
        grade_head = head_cols(grade_block, head)
        scores = right_contract(query_head, key_head) * HD ** (-0.5)
        probability = jnp.exp(scores - logsum[head][:, None])
        value_parts.append(left_contract(probability.astype(jnp.bfloat16), grade_head))
        prob_grad = right_contract(grade_head, head_cols(value_block, head))
        score_grad = probability * (
            prob_grad - jnp.sum(probability * prob_grad, axis=-1, keepdims=True)
        )
        score_low = score_grad.astype(jnp.bfloat16)
        query_parts.append(matmul(score_low, key_head) * HD ** (-0.5))
        key_parts.append(left_contract(score_low, query_head) * HD ** (-0.5))
    return [
        jnp.concatenate(parts, axis=1).astype(jnp.bfloat16)
        for parts in (query_parts, key_parts, value_parts)
    ]


MESH = pl.DeviceIdType.MESH
PARAMS = dict(has_side_effects=True, vmem_limit_bytes=40 * 1024 * 1024)


def greet(groups):
    barrier = pltpu.get_barrier_semaphore()
    count = 0
    for axis, peers in groups:
        for peer in peers:
            pl.semaphore_signal(barrier, inc=1, device_id={axis: peer}, device_id_type=MESH)
            count += 1
    pl.semaphore_wait(barrier, count)


def remote(src, dst, sems, slot, axis, peer):
    copy = pltpu.make_async_remote_copy(
        src_ref=src,
        dst_ref=dst,
        send_sem=sems.at[0, slot],
        recv_sem=sems.at[1, slot],
        device_id={axis: peer},
        device_id_type=MESH,
    )
    copy.start()
    return copy


def exchange_kernel(n_t, n_d, n_gather, n_reduce, n_dp, *refs):
    refs = list(refs)

    def take(count):
        taken = refs[:count]
        del refs[:count]
        return taken

    gather_in, reduce_in, dp_in = take(n_gather), take(n_reduce), take(n_dp)
    gather_out, reduce_out, dp_out = take(n_gather), take(n_reduce), take(n_dp)
    gather_sems = take(n_gather)
    reduce_scratch = [take(2) for _ in range(n_reduce)]
    dp_scratch = [take(5) for _ in range(n_dp)]
    rank = lax.axis_index("tensor")
    t_peers = [lax.rem(rank + k, n_t) for k in range(1, n_t)]
    groups = [("tensor", t_peers)]
    n_chip = n_d // 2
    if n_dp:
        place = lax.axis_index("dp")
        chip = place // 2
        core = lax.rem(place, 2)
        chips = [lax.rem(chip + k, n_chip) for k in range(n_chip)]
        sibling = chip * 2 + 1 - core
        d_peers = [chips[k] * 2 + core for k in range(1, n_chip)]
        groups.append(("dp", [sibling] + d_peers))
    greet(groups)
    order = list(range(1, n_chip)) + [0]
    pending = []
    first_phase = []
    for src, (near, outgoing, far, near_sems, far_sems) in zip(dp_in, dp_scratch):
        first_phase.append(
            {
                k: remote(src.at[chips[k], 1 - core], near.at[k], near_sems, k, "dp", sibling)
                for k in order
            }
        )
    gathers = []
    for src, dst, sems in zip(gather_in, gather_out, gather_sems):
        rows = src.shape[0]
        own = pl.ds(pl.multiple_of(rank * rows, rows), rows)
        for k, peer in enumerate(t_peers):
            gathers.append(remote(src, dst.at[own], sems, k, "tensor", peer))
    reduces = []
    for src, (landed, sems) in zip(reduce_in, reduce_scratch):
        rows = landed.shape[1]
        copies = []
        for k, peer in enumerate(t_peers):
            part = pl.ds(pl.multiple_of(peer * rows, rows), rows)
            copies.append(remote(src.at[part], landed.at[k], sems, k, "tensor", peer))
        reduces.append(copies)
    second_phase = []
    for src, out, copies, (near, outgoing, far, near_sems, far_sems) in zip(
        dp_in, dp_out, first_phase, dp_scratch
    ):
        later = []
        for k in order:
            copies[k].wait_recv()
            value = src[chips[k], core].astype(jnp.float32) + near[k].astype(jnp.float32)
            if k == 0:
                out[...] = value
            else:
                outgoing[k - 1] = value.astype(outgoing.dtype)
                later.append(
                    remote(
                        outgoing.at[k - 1], far.at[k - 1], far_sems, k - 1, "dp", d_peers[k - 1]
                    )
                )
        second_phase.append(later)
    for src, dst in zip(gather_in, gather_out):
        rows = src.shape[0]
        dst[pl.ds(pl.multiple_of(rank * rows, rows), rows), :] = src[...]
    for src, out, copies, (landed, sems) in zip(reduce_in, reduce_out, reduces, reduce_scratch):
        rows = landed.shape[1]
        total = src[pl.ds(pl.multiple_of(rank * rows, rows), rows), :].astype(jnp.float32)
        for k, copy in enumerate(copies):
            copy.wait_recv()
            total = total + landed[k].astype(jnp.float32)
        out[...] = total
    for copy in gathers:
        copy.wait_recv()
    for out, later, scratch in zip(dp_out, second_phase, dp_scratch):
        total = out[...]
        for k, copy in enumerate(later):
            copy.wait_recv()
            total = total + scratch[2][k].astype(jnp.float32)
        out[...] = total
    for copy in gathers:
        copy.wait_send()
    for copies in reduces + second_phase:
        for copy in copies:
            copy.wait_send()
    for copies in first_phase:
        for k in order:
            copies[k].wait_send()


def exchange(ident, gathers=(), reduces=(), dp_reduces=()):
    n_t, n_d = lax.axis_size("tensor"), lax.axis_size("dp")
    n_chip = n_d // 2
    outs = []
    scratch = []
    by_kernel = n_d <= 8 and n_d % 2 == 0
    inputs = list(gathers) + list(reduces)
    for value in gathers:
        outs.append(jax.ShapeDtypeStruct((n_t * value.shape[0], value.shape[1]), value.dtype))
        scratch.append(pltpu.SemaphoreType.DMA((2, n_t - 1)))
    for value in reduces:
        rows, columns = value.shape[0] // n_t, value.shape[1]
        outs.append(jax.ShapeDtypeStruct((rows, columns), jnp.float32))
        scratch.append(pltpu.VMEM((n_t - 1, rows, columns), value.dtype))
        scratch.append(pltpu.SemaphoreType.DMA((2, n_t - 1)))
    n_dp = 0
    if by_kernel:
        for value in dp_reduces:
            rows, columns = value.shape[0] // n_d, value.shape[1]
            n_dp += 1
            inputs.append(value.reshape(n_chip, 2, rows, columns))
            outs.append(jax.ShapeDtypeStruct((rows, columns), jnp.float32))
            scratch += [
                pltpu.VMEM((n_chip, rows, columns), value.dtype),
                pltpu.VMEM((n_chip - 1, rows, columns), value.dtype),
                pltpu.VMEM((n_chip - 1, rows, columns), value.dtype),
                pltpu.SemaphoreType.DMA((2, n_chip)),
                pltpu.SemaphoreType.DMA((2, n_chip - 1)),
            ]
    results = pl.pallas_call(
        partial(exchange_kernel, n_t, n_d, len(gathers), len(reduces), n_dp),
        out_shape=outs,
        in_specs=[pl.BlockSpec(memory_space=pltpu.VMEM)] * len(inputs),
        out_specs=[pl.BlockSpec(memory_space=pltpu.VMEM)] * len(outs),
        scratch_shapes=scratch,
        compiler_params=pltpu.CompilerParams(collective_id=ident, **PARAMS),
        name="exchange_%d" % ident,
    )(*inputs)
    if not by_kernel:
        results = list(results) + [
            lax.psum_scatter(value.astype(jnp.float32), "dp", scatter_dimension=0, tiled=True)
            for value in dp_reduces
        ]
    return results


def vector_kernel(n_t, n_d, first, shares, first_all, share_all, landed, total, *sems):
    first_sems, part_sems, total_sems = sems
    rank, place = lax.axis_index("tensor"), lax.axis_index("dp")
    t_peers = [lax.rem(rank + k, n_t) for k in range(1, n_t)]
    d_peers = [lax.rem(place + k, n_d) for k in range(1, n_d)]
    greet([("tensor", t_peers), ("dp", d_peers)])
    parts = [
        remote(shares.at[peer], landed.at[k], part_sems, k, "tensor", peer)
        for k, peer in enumerate(t_peers)
    ]
    copies = [
        remote(first, first_all.at[place], first_sems, k, "dp", peer)
        for k, peer in enumerate(d_peers)
    ]
    value = shares[rank]
    for k, copy in enumerate(parts):
        copy.wait_recv()
        value = value + landed[k]
    total[...] = value
    copies += [
        remote(total, share_all.at[place], total_sems, k, "dp", peer)
        for k, peer in enumerate(d_peers)
    ]
    share_all[place] = value
    first_all[place] = first[...]
    for copy in copies:
        copy.wait_recv()
    for copy in copies + parts:
        copy.wait_send()


def gather_vectors(ident, first, shares):
    n_t, n_d = lax.axis_size("tensor"), lax.axis_size("dp")
    if n_d > 8:
        total = lax.psum_scatter(shares, "tensor", scatter_dimension=0, tiled=True)
        return (lax.all_gather(first, "dp"), lax.all_gather(total, "dp"))
    length, width = first.shape[0], shares.shape[0] // n_t
    length_rows, width_rows = -(-length // 1024) * 8, -(-width // 1024) * 8
    first = jnp.pad(first, (0, length_rows * 128 - length)).reshape(length_rows, 128)
    shares = jnp.pad(shares.reshape(n_t, width), ((0, 0), (0, width_rows * 128 - width)))
    shares = shares.reshape(n_t, width_rows, 128)
    first_all, share_all = pl.pallas_call(
        partial(vector_kernel, n_t, n_d),
        out_shape=[
            jax.ShapeDtypeStruct((n_d, length_rows, 128), jnp.float32),
            jax.ShapeDtypeStruct((n_d, width_rows, 128), jnp.float32),
        ],
        in_specs=[pl.BlockSpec(memory_space=pltpu.VMEM)] * 2,
        out_specs=[pl.BlockSpec(memory_space=pltpu.VMEM)] * 2,
        scratch_shapes=[
            pltpu.VMEM((n_t - 1, width_rows, 128), jnp.float32),
            pltpu.VMEM((width_rows, 128), jnp.float32),
            pltpu.SemaphoreType.DMA((2, n_d - 1)),
            pltpu.SemaphoreType.DMA((2, n_t - 1)),
            pltpu.SemaphoreType.DMA((2, n_d - 1)),
        ],
        compiler_params=pltpu.CompilerParams(collective_id=ident, **PARAMS),
        name="gather_vectors",
    )(first, shares)
    return (
        first_all.reshape(n_d, -1)[:, :length],
        share_all.reshape(n_d, -1)[:, :width],
    )


def local(
    tokens,
    condition,
    modulate_weight,
    modulate_bias,
    heads_weight,
    heads_bias,
    output_weight,
    output_bias,
    first_weight,
    first_bias,
    second_weight,
    second_bias,
    cotangent,
):
    row_count, model_width = tokens.shape
    n_t, n_d = lax.axis_size("tensor"), lax.axis_size("dp")
    local_width = heads_weight.shape[2]
    assert condition.shape[0] == 1 and n_t * row_count == LEN
    low = jnp.bfloat16
    silu_cond = jax.nn.silu(condition.astype(jnp.float32)).astype(low)
    modulate_local = matmul(silu_cond, modulate_weight) + modulate_bias
    mod_width = modulate_local.shape[1]
    mod_rows = -(-mod_width // 1024) * 8
    padded = jnp.pad(modulate_local[0], (0, mod_rows * 128 - mod_width)).reshape(mod_rows, 128)
    (modulation,) = exchange(0, gathers=[padded])
    modulation = modulation.reshape(n_t, mod_rows * 128)[:, :mod_width].reshape(1, -1)
    pieces = [
        modulation[:, member * model_width : (member + 1) * model_width] for member in range(6)
    ]
    shift_attn, scale_attn, gate_attn, shift_feed, scale_feed, gate_feed = pieces
    residual = tokens.astype(jnp.float32)
    tangent = cotangent.astype(jnp.float32)
    normed_first, inverse_first = layer_norm(residual)
    attention_in = (normed_first * (1.0 + scale_attn) + shift_attn).astype(low)
    feed_grad = (gate_feed * tangent).astype(low)
    attention_all, feed_grad_all = exchange(1, gathers=[attention_in, feed_grad])
    query_rows = (matmul(attention_all, heads_weight[0]) + heads_bias[0]).astype(low)
    key_rows = matmul(attention_all, heads_weight[1]).astype(low)
    value_rows = (matmul(attention_all, heads_weight[2]) + heads_bias[1]).astype(low)
    mixture, logsum = attend_forward((query_rows, key_rows, value_rows))
    (branch_attn,) = exchange(2, reduces=[matmul(mixture, output_weight).astype(low)])
    branch_attn = branch_attn + output_bias
    residual_mid = residual + gate_attn * branch_attn
    normed_second, inverse_second = layer_norm(residual_mid)
    feed_in = (normed_second * (1.0 + scale_feed) + shift_feed).astype(low)
    (feed_all,) = exchange(3, gathers=[feed_in])
    hidden_pre = matmul(feed_all, first_weight) + first_bias
    activated, gelu_back = jax.vjp(partial(jax.nn.gelu, approximate=True), hidden_pre)
    activated = activated.astype(low)
    activated_grad = right_contract(feed_grad_all, second_weight)
    pre_grad = gelu_back(activated_grad)[0].astype(low)
    feed_in_grad, branch_feed = exchange(
        4,
        reduces=[
            right_contract(pre_grad, first_weight).astype(low),
            matmul(activated, second_weight).astype(low),
        ],
    )
    branch_feed = branch_feed + second_bias
    output = (residual_mid + gate_feed * branch_feed).astype(low)
    mid_grad = tangent + norm_back(feed_in_grad * (1.0 + scale_feed), normed_second, inverse_second)
    attn_grad = (gate_attn * mid_grad).astype(low)
    attn_grad_all, first_share, second_share = exchange(
        5,
        gathers=[attn_grad],
        dp_reduces=[
            left_contract(feed_all, pre_grad).astype(low),
            left_contract(feed_grad_all, activated).astype(low),
        ],
    )
    mixture_grad = right_contract(attn_grad_all, output_weight).astype(low)
    heads_grad = attend_backward((query_rows, key_rows, value_rows, mixture_grad, logsum))
    attn_in_partial = sum(right_contract(heads_grad[s], heads_weight[s]) for s in range(3))
    inner_grads = jnp.concatenate(
        [left_contract(attention_all, part).astype(low) for part in heads_grad]
        + [left_contract(attn_grad_all, mixture).astype(low)],
        axis=1,
    )
    attn_in_grad, inner_share = exchange(
        6, reduces=[attn_in_partial.astype(low)], dp_reduces=[inner_grads]
    )
    token_grad = mid_grad + norm_back(
        attn_in_grad * (1.0 + scale_attn), normed_first, inverse_first
    )
    modulation_partial = jnp.concatenate(
        [
            jnp.sum(term, axis=0)
            for term in (
                attn_in_grad,
                attn_in_grad * normed_first,
                mid_grad * branch_attn,
                feed_in_grad,
                feed_in_grad * normed_second,
                tangent * branch_feed,
            )
        ]
    )
    columns = [heads_grad[0], heads_grad[2], attn_grad_all, pre_grad, feed_grad_all]
    sums = [jnp.sum(value, axis=0, dtype=jnp.float32) for value in columns]
    vectors, modulation_all = gather_vectors(
        7, jnp.concatenate(sums + [silu_cond[0].astype(jnp.float32)]), modulation_partial
    )
    bias_total = jnp.sum(vectors, axis=0)
    offsets = [0]
    for value in sums:
        offsets.append(offsets[-1] + value.shape[0])
    bias_grads = [bias_total[offsets[i] : offsets[i + 1]] for i in range(5)]
    share = model_width // n_d
    cond_share = lax.dynamic_slice_in_dim(
        vectors[:, offsets[-1] :], lax.axis_index("dp") * share, share, 1
    )
    grad_modulate_weight = exact_left(cond_share, modulation_all)
    heads_share = inner_share[:, : 3 * local_width].reshape(share, 3, local_width)
    return (
        output,
        token_grad,
        grad_modulate_weight,
        jnp.sum(modulation_all, axis=0),
        jnp.swapaxes(heads_share, 0, 1),
        jnp.stack(bias_grads[:2]),
        inner_share[:, 3 * local_width :].T,
        bias_grads[2],
        first_share,
        bias_grads[3],
        second_share.T,
        bias_grads[4],
    )


def solution(mesh):
    in_specs = (
        P(("dp", "tensor"), None),
        P("dp", None),
        P(None, "tensor"),
        P("tensor"),
        P(None, None, "tensor"),
        P(None, "tensor"),
        P("tensor", None),
        P(),
        P(None, "tensor"),
        P("tensor"),
        P("tensor", None),
        P(),
        P(("dp", "tensor"), None),
    )
    out_specs = (
        P(("dp", "tensor"), None),
        P(("dp", "tensor"), None),
        P("dp", "tensor"),
        P("tensor"),
        P(None, "dp", "tensor"),
        P(None, "tensor"),
        P("tensor", "dp"),
        P(),
        P("dp", "tensor"),
        P("tensor"),
        P("tensor", "dp"),
        P(),
    )
    return jax.shard_map(local, mesh=mesh, in_specs=in_specs, out_specs=out_specs, check_vma=False)
```

time: 489 us -> 230 us (0.47)
  waiting for transfers between devices: 264 us -> 0 us
  Pallas kernels: 0 us -> 167 us
  blocking collectives: 128 us -> 0 us
  between operations: 14.8 us -> 1.57 us
  matrix products: 38.3 us -> 26.3 us
    pallas_call x0 -> x8, Pallas kernels: none -> 167 us  [the longest x7 155 us: exchange(): pl.pallas_call(partial(exchange_kernel, n_t, n_d, len(gathers), len(reduc...]
    reduce_scatter x6 -> x0, waiting for transfers between devices: 164 us -> none  [the longest x1 46.5 us: local(): lax.psum_scatter(grad_first_weight, 'dp', scatter_dimension=0, tiled=True)]
    all_gather x7 -> x0, blocking collectives: 104 us -> none  [the longest x1 18.3 us: local(): attn_grad_all = lax.all_gather(attn_grad, 'tensor', axis=0, tiled=True)]
    unnamed x12 -> x0, waiting for transfers between devices: 99.9 us -> none
    psum x1 -> x0, blocking collectives: 24.4 us -> none  [local(): lax.psum((grad_modulate_bias, grad_heads_bias, grad_output_bias, grad_fir...]
    unnamed x143 -> x103, local copies, waits for them, and re-layouts: 21.3 us -> 11.7 us
    unnamed x3 -> x0, matrix products: 5.57 us -> none
    dot_general x2 -> x0, matrix products: 5.23 us -> none  [the longest x1 3.19 us: local(): jnp.einsum('td,ste->sde', attention_all, heads_grad, preferred_element_ty...]
  transfers between devices with their start and end apart: 9 -> 0, of which waited for: 9 -> 0; matrix products, arithmetic and copies ran while one was open for 9% -> 0% of each run, Pallas kernels for 0% -> 0%
where the time goes in v1:
time: 230 us; the launch traced here: 229 us
  Pallas kernels  167 us (73%)
  matrix products  26.3 us (11%)
  local copies, waits for them, and re-layouts  19.1 us (8%)
  other arithmetic  15.4 us (7%)
    pallas_call x7, Pallas kernels, exchange(): pl.pallas_call(partial(exchange_kernel, n_t, n_d, len(gathers), len(reduc...  155 us
    unnamed x103, local copies, waits for them, and re-layouts  11.7 us
    pallas_call x1, Pallas kernels, gather_vectors(): pl.pallas_call(partial(vector_kernel, n_t, n_d), out_shape=[jax.ShapeDtyp...  11.5 us
    dot_general x12, matrix products, left_contract(): lax.dot_general(left, right, (((0,), (0,)), ((), ())), preferred_element_...  10 us
    dot_general x13, matrix products, matmul(): return jnp.dot(left, right, preferred_element_type=jnp.float32)  8.51 us
    dot_general x12, matrix products, right_contract(): lax.dot_general(left, right, (((1,), (1,)), ((), ())), preferred_element_...  6.44 us

profile of v1, /device:TPU:0, one launch (start us, length us, event | category | flops | bytes accessed | tf_op | source)
XLA Modules:
  0.0 229.2 jit_solution(5822349233143197565)
XLA Ops:
  0.7 1.2 convert_reduce_fusion.3
  1.9 1.1 fusion.40
  3.0 1.3 convert_reduce_fusion.6
  5.1 1.0 convolution_reduce_fusion
  6.2 7.4 %exchange_0.1 = f32[64,128]{1,0:T(8,128)S(1)} custom-call(f32[16,128]{1,0:T(8,128)S(1)} %pad_bitcast_fusion.2.refs_0_), custom_call_target="tpu_custom_call" | custom-call | tf_op jit(solution)/shard_map/exchange_0/pallas_call | solution.py:256
  14.0 33.1 %exchange_1.1 = (bf16[512,768]{1,0:T(8,128)(2,1)S(1)}, bf16[512,768]{1,0:T(8,128)(2,1)S(1)}) custom-call(bf16[128,768]{1,0:T(8,128)(2,1)S(1)} %get-tuple-element.102.refs_0_, bf16[128,768]{1,0:T(8,128)(2,1)S(1)} %get-tuple-element.103.refs_1_), custom_call_target="tpu_custom_call" | custom-call | tf_op jit(solution)/shard_map/exchange_1/pallas_call | solution.py:256
  47.8 1.4 fusion.8
  53.8 20.4 %exchange_2.1 = f32[128,768]{1,0:T(8,128)S(1)} custom-call(bf16[512,768]{1,0:T(8,128)(2,1)S(1)} %convolution_convert_fusion.4.refs_0_), custom_call_target="tpu_custom_call" | custom-call | tf_op jit(solution)/shard_map/exchange_2/pallas_call | solution.py:256
  74.7 18.6 %exchange_3.1 = bf16[512,768]{1,0:T(8,128)(2,1)S(1)} custom-call(bf16[128,768]{1,0:T(8,128)(2,1)S(1)} %add_convert_fusion.2.refs_0_), custom_call_target="tpu_custom_call" | custom-call | tf_op jit(solution)/shard_map/exchange_3/pallas_call | solution.py:256
  94.6 2.3 convert_reduce_fusion.1
  99.4 1.1 convolution_convert_fusion.2.refs_1_
  100.5 35.6 %exchange_4.1 = (f32[128,768]{1,0:T(8,128)S(1)}, f32[128,768]{1,0:T(8,128)S(1)}) custom-call(bf16[512,768]{1,0:T(8,128)(2,1)S(1)} %convolution_convert_fusion.3.refs_0_, bf16[512,768]{1,0:T(8,128)(2,1)S(1)} %convolution_convert_fusion.2.refs_1_), custom_call_target="tpu_custom_call" | custom-call | tf_op jit(solution)/shard_map/exchange_4/pallas_call | solution.py:256
  136.9 1.7 fusion.42
  139.6 19.9 %exchange_5.1 = (bf16[512,768]{1,0:T(8,128)(2,1)S(1)}, f32[96,768]{1,0:T(8,128)S(1)}, f32[96,768]{1,0:T(8,128)S(1)}) custom-call(bf16[128,768]{1,0:T(8,128)(2,1)S(1)} %multiply_convert_fusion.4.refs_0_, bf16[4,2,96,768]{3,2,1,0:T(8,128)(2,1)S(1)} %bitcast.80, bf16[4,2,96,768]{3,2,1,0:T(8,128)(2,1)S(1)} %bitcast.81), custom_call_target="tpu_custom_call" | custom-call | tf_op jit(solution)/shard_map/exchange_5/pallas_call | solution.py:256
  159.7 1.2 convolution_convert_fusion.5
  162.9 1.0 convolution_convert_fusion.6
  169.5 1.4 concatenate.30
  171.6 1.2 convolution_convert_fusion.7
  172.8 1.2 convolution_convert_fusion.8
  174.0 1.1 pad_maximum_fusion
  175.1 1.6 copy.28
  176.8 1.4 fusion.48
  179.2 20.3 %exchange_6.1 = (f32[128,768]{1,0:T(8,128)S(1)}, f32[96,768]{1,0:T(8,128)S(1)}) custom-call(bf16[512,768]{1,0:T(8,128)(2,1)S(1)} %add_convert_fusion.refs_0_, bf16[4,2,96,768]{3,2,1,0:T(8,128)(2,1)S(1)} %bitcast.79), custom_call_target="tpu_custom_call" | custom-call | tf_op jit(solution)/shard_map/exchange_6/pallas_call | solution.py:256
  200.5 1.3 constant_dynamic-update-slice_fusion.5
  201.8 1.3 constant_dynamic-update-slice_fusion.4
  203.1 1.3 constant_dynamic-update-slice_fusion.3
  204.4 1.3 constant_dynamic-update-slice_fusion.2
  205.7 1.3 constant_dynamic-update-slice_fusion.1
  207.0 1.3 constant_dynamic-update-slice_fusion
  209.0 1.9 fusion.38
  212.9 11.5 %gather_vectors.1 = (f32[8,32,128]{2,1,0:T(8,128)S(1)}, f32[8,16,128]{2,1,0:T(8,128)S(1)}) custom-call(f32[32,128]{1,0:T(8,128)S(1)} %pad_bitcast_fusion.1.first, f32[4,16,128]{2,1,0:T(8,128)S(1)} %bitcast.84), custom_call_target="tpu_custom_call" | custom-call | tf_op jit(solution)/shard_map/gather_vectors/pallas_call | solution.py:314
  226.4 1.4 fusion.84
  (171 shorter events, 28.6 us)
Async XLA Ops:
  0.6 4.5 %copy-start = (bf16[768,1152]{1,0:T(8,128)(2,1)S(1)}, bf16[768,1152]{1,0:T(8,128)(2,1)}, u32[]{:S(2)}) copy-start(bf16[768,1152]{1,0:T(8,128)(2,1)} %param.15) | copy-start | bytes 5308420
  0.7 13.1 %copy-start.7 = (bf16[128,768]{1,0:T(8,128)(2,1)S(1)}, bf16[128,768]{1,0:T(8,128)(2,1)}, u32[]{:S(2)}) copy-start(bf16[128,768]{1,0:T(8,128)(2,1)} %param.13) | copy-start | bytes 589828
  0.7 13.1 %copy-start.10 = (bf16[128,768]{1,0:T(8,128)(2,1)S(1)}, bf16[128,768]{1,0:T(8,128)(2,1)}, u32[]{:S(2)}) copy-start(bf16[128,768]{1,0:T(8,128)(2,1)} %param.25) | copy-start | bytes 589828
  0.7 5.5 %copy-start.36 = (f32[1152]{0:T(1024)S(1)}, f32[1152]{0:T(1024)}, u32[]{:S(2)}) copy-start(f32[1152]{0:T(1024)} %param.16) | copy-start | bytes 13828
  1.9 45.2 %copy-start.34 = (f32[128]{0:T(128)}, f32[128]{0:T(128)S(1)}, u32[]{:S(2)}) copy-start(f32[128]{0:T(128)S(1)} %broadcast_multiply_fusion.5) | copy-start | bytes 1540
  3.0 44.0 %copy-start.38 = (f32[128]{0:T(128)}, f32[128]{0:T(128)S(1)}, u32[]{:S(2)}) copy-start(f32[128]{0:T(128)S(1)} %add_rsqrt_fusion.1) | copy-start | bytes 1540
  13.7 35.5 %copy-start.26 = (f32[768]{0:T(1024)}, f32[768]{0:T(1024)S(1)}, u32[]{:S(2)}) copy-start(f32[768]{0:T(1024)S(1)} %get-tuple-element.70) | copy-start | bytes 9220
  13.8 35.4 %copy-start.8 = (bf16[3,768,192]{1,2,0:T(8,128)(2,1)S(1)}, bf16[3,768,192]{1,2,0:T(8,128)(2,1)}, u32[]{:S(2)}) copy-start(bf16[3,768,192]{1,2,0:T(8,128)(2,1)} %param.17) | copy-start | bytes 2654212
  53.4 20.9 %copy-start.28 = (f32[768]{0:T(1024)S(1)}, f32[768]{0:T(1024)}, u32[]{:S(2)}) copy-start(f32[768]{0:T(1024)} %param.20) | copy-start | bytes 9220
  74.2 19.1 %copy-start.42 = (bf16[768,768]{1,0:T(8,128)(2,1)S(1)}, bf16[768,768]{1,0:T(8,128)(2,1)}, u32[]{:S(2)}) copy-start(bf16[768,768]{1,0:T(8,128)(2,1)} %param.23) | copy-start | bytes 3538948
  100.5 36.4 %copy-start.40 = (f32[768]{0:T(1024)S(1)}, f32[768]{0:T(1024)}, u32[]{:S(2)}) copy-start(f32[768]{0:T(1024)} %param.24) | copy-start | bytes 9220
  159.5 1.8 copy-start.3
  159.5 1.8 copy-start.5
  161.9 2.4 %copy-start.11 = (bf16[512,64]{0,1:T(8,128)(2,1)}, bf16[512,64]{0,1:T(8,128)(2,1)S(1)}, u32[]{:S(2)}) copy-start(bf16[512,64]{0,1:T(8,128)(2,1)S(1)} %convolution_convert_fusion.15) | copy-start | bytes 196612
  162.2 2.1 copy-start.13
  164.8 4.5 %copy-start.15 = (bf16[512,64]{0,1:T(8,128)(2,1)}, bf16[512,64]{0,1:T(8,128)(2,1)S(1)}, u32[]{:S(2)}) copy-start(bf16[512,64]{0,1:T(8,128)(2,1)S(1)} %fusion.14) | copy-start | bytes 196612
  166.6 2.7 %copy-start.17 = (bf16[512,64]{0,1:T(8,128)(2,1)}, bf16[512,64]{0,1:T(8,128)(2,1)S(1)}, u32[]{:S(2)}) copy-start(bf16[512,64]{0,1:T(8,128)(2,1)S(1)} %fusion.13) | copy-start | bytes 196612
  167.9 3.7 %copy-start.22 = (bf16[512,64]{0,1:T(8,128)(2,1)S(1)}, bf16[512,64]{0,1:T(8,128)(2,1)}, u32[]{:S(2)}) copy-start(bf16[512,64]{0,1:T(8,128)(2,1)} %fusion.11) | copy-start | bytes 196612
  169.3 4.7 %copy-start.19 = (bf16[768,192]{0,1:T(8,128)(2,1)S(1)}, bf16[768,192]{0,1:T(8,128)(2,1)}, u32[]{:S(2)}) copy-start(bf16[768,192]{0,1:T(8,128)(2,1)} %convolution_convert_fusion.5) | copy-start | bytes 884740
  169.3 4.7 %copy-start.20 = (bf16[768,192]{0,1:T(8,128)(2,1)S(1)}, bf16[768,192]{0,1:T(8,128)(2,1)}, u32[]{:S(2)}) copy-start(bf16[768,192]{0,1:T(8,128)(2,1)} %convolution_convert_fusion.6) | copy-start | bytes 884740
  176.8 1.9 copy-start.12
  176.8 1.9 copy-start.14
  179.1 21.1 %copy-start.27 = (f32[768]{0:T(1024)S(1)}, f32[768]{0:T(1024)}, u32[]{:S(2)}) copy-start(f32[768]{0:T(1024)} %copy-done.26) | copy-start | bytes 9220
  179.2 21.1 %copy-start.35 = (f32[128]{0:T(128)S(1)}, f32[128]{0:T(128)}, u32[]{:S(2)}) copy-start(f32[128]{0:T(128)} %copy-done.34) | copy-start | bytes 1540
  179.2 21.1 %copy-start.39 = (f32[128]{0:T(128)S(1)}, f32[128]{0:T(128)}, u32[]{:S(2)}) copy-start(f32[128]{0:T(128)} %copy-done.38) | copy-start | bytes 1540
  179.2 23.9 %copy-start.32 = (f32[768]{0:T(1024)S(1)}, f32[768]{0:T(1024)}, u32[]{:S(2)}) copy-start(f32[768]{0:T(1024)} %get-tuple-element.80) | copy-start | bytes 9220
  179.2 25.2 %copy-start.30 = (f32[768]{0:T(1024)S(1)}, f32[768]{0:T(1024)}, u32[]{:S(2)}) copy-start(f32[768]{0:T(1024)} %get-tuple-element.64) | copy-start | bytes 9220
  179.2 26.5 %copy-start.29 = (f32[768]{0:T(1024)S(1)}, f32[768]{0:T(1024)}, u32[]{:S(2)}) copy-start(f32[768]{0:T(1024)} %get-tuple-element.58) | copy-start | bytes 9220
  179.2 27.8 %copy-start.31 = (f32[768]{0:T(1024)S(1)}, f32[768]{0:T(1024)}, u32[]{:S(2)}) copy-start(f32[768]{0:T(1024)} %get-tuple-element.78) | copy-start | bytes 9220
  200.2 10.7 %copy-start.2 = (f32[96,768]{1,0:T(8,128)S(1)}, f32[96,768]{1,0:T(8,128)}, u32[]{:S(2)}) copy-start(f32[96,768]{1,0:T(8,128)} %copy-done.1) | copy-start | bytes 884740
  211.0 16.8 %copy-start.6 = (f32[96,768]{1,0:T(8,128)S(1)}, f32[96,768]{1,0:T(8,128)}, u32[]{:S(2)}) copy-start(f32[96,768]{1,0:T(8,128)} %copy-done.5) | copy-start | bytes 884740
  211.1 17.4 %copy-start.4 = (f32[96,768]{1,0:T(8,128)S(1)}, f32[96,768]{1,0:T(8,128)}, u32[]{:S(2)}) copy-start(f32[96,768]{1,0:T(8,128)} %copy-done.3) | copy-start | bytes 884740
  (12 other events, 16.8 us)

commit v2 on v1

--- a/solution.py
+++ b/solution.py
@@ -128,6 +128,149 @@
     return copy
 
 
+PIECES = 2
+
+
+def signs(rank, n_t):
+    return (
+        (0, 1, rank + 1 < n_t, rank > 0),
+        (1, -1, rank > 0, rank + 1 < n_t),
+    )
+
+
+def line_copy(src, dst, sems, way, slot, piece, peer):
+    return pltpu.make_async_remote_copy(
+        src_ref=src,
+        dst_ref=dst,
+        send_sem=sems.at[0, way, slot, piece],
+        recv_sem=sems.at[1, way, slot, piece],
+        device_id={"tensor": peer},
+        device_id_type=MESH,
+    )
+
+
+def inside(index, n_t):
+    return jnp.logical_and(index >= 0, index < n_t)
+
+
+def gather_step(rank, n_t, distance, items):
+    for piece in range(PIECES):
+        for way, step, ahead, behind in signs(rank, n_t):
+            origin = rank - step * distance
+            for src, out, sems in items:
+                half = src.shape[0] // PIECES
+                rows = pl.ds(pl.multiple_of(origin * src.shape[0] + piece * half, half), half)
+                block = out.at[rows]
+                if distance:
+
+                    @pl.when(inside(origin, n_t))
+                    def _():
+                        line_copy(
+                            block, block, sems, way, distance - 1, piece, rank - step
+                        ).wait_recv()
+
+                if distance < n_t - 1:
+
+                    @pl.when(jnp.logical_and(inside(origin, n_t), ahead))
+                    def _():
+                        held = block if distance else src.at[pl.ds(piece * half, half)]
+                        line_copy(held, block, sems, way, distance, piece, rank + step).start()
+
+
+def gather_finish(rank, n_t, items):
+    for distance in range(n_t - 1):
+        for piece in range(PIECES):
+            for way, step, ahead, behind in signs(rank, n_t):
+                origin = rank - step * distance
+                for src, out, sems in items:
+                    half = src.shape[0] // PIECES
+                    rows = pl.ds(pl.multiple_of(origin * src.shape[0] + piece * half, half), half)
+
+                    @pl.when(jnp.logical_and(inside(origin, n_t), ahead))
+                    def _():
+                        held = out.at[rows] if distance else src.at[pl.ds(piece * half, half)]
+                        line_copy(
+                            held, out.at[rows], sems, way, distance, piece, rank + step
+                        ).wait_send()
+
+
+def reduce_step(rank, n_t, items, stage):
+    for distance in range(n_t - 1, 0, -1):
+        for piece in range(PIECES):
+            for way, step, ahead, behind in signs(rank, n_t):
+                target = rank + step * distance
+                for src, landed, outgoing, sems in items:
+                    whole = landed.shape[2]
+                    half = whole // PIECES
+                    rows = pl.ds(pl.multiple_of(target * whole + piece * half, half), half)
+                    part = pl.ds(piece * half, half)
+                    slot = distance - 1
+                    ends = jnp.logical_and(inside(target, n_t), jnp.logical_not(behind))
+                    inner = jnp.logical_and(inside(target, n_t), behind)
+
+                    def make(first):
+                        return line_copy(
+                            src.at[rows] if first else outgoing.at[way, slot, part],
+                            landed.at[way, slot, part],
+                            sems,
+                            way,
+                            slot,
+                            piece,
+                            rank + step,
+                        )
+
+                    if stage == 0:
+
+                        @pl.when(ends)
+                        def _():
+                            make(True).start()
+
+                    if stage == 1 and distance < n_t - 1:
+
+                        @pl.when(inner)
+                        def _():
+                            arrived = landed.at[way, distance, part]
+                            line_copy(
+                                arrived, arrived, sems, way, distance, piece, rank - step
+                            ).wait_recv()
+                            outgoing[way, slot, part, :] = (
+                                src[rows, :].astype(jnp.float32)
+                                + landed[way, distance, part, :].astype(jnp.float32)
+                            ).astype(outgoing.dtype)
+                            make(False).start()
+
+                    if stage == 2:
+
+                        @pl.when(ends)
+                        def _():
+                            make(True).wait_send()
+
+                        if distance < n_t - 1:
+
+                            @pl.when(inner)
+                            def _():
+                                make(False).wait_send()
+
+
+def reduce_total(rank, n_t, items, outs):
+    for (src, landed, outgoing, sems), out in zip(items, outs):
+        whole = landed.shape[2]
+        half = whole // PIECES
+        own = pl.ds(pl.multiple_of(rank * whole, whole), whole)
+        out[...] = src[own, :].astype(jnp.float32)
+    for piece in range(PIECES):
+        for way, step, ahead, behind in signs(rank, n_t):
+            for (src, landed, outgoing, sems), out in zip(items, outs):
+                half = landed.shape[2] // PIECES
+                part = pl.ds(piece * half, half)
+
+                @pl.when(behind)
+                def _():
+                    arrived = landed.at[way, 0, part]
+                    line_copy(arrived, arrived, sems, way, 0, piece, rank - step).wait_recv()
+                    out[part, :] = out[part, :] + landed[way, 0, part, :].astype(jnp.float32)
+
+
 def exchange_kernel(n_t, n_d, n_gather, n_reduce, n_dp, *refs):
     refs = list(refs)
 
@@ -139,7 +282,7 @@
     gather_in, reduce_in, dp_in = take(n_gather), take(n_reduce), take(n_dp)
     gather_out, reduce_out, dp_out = take(n_gather), take(n_reduce), take(n_dp)
     gather_sems = take(n_gather)
-    reduce_scratch = [take(2) for _ in range(n_reduce)]
+    reduce_scratch = [take(3) for _ in range(n_reduce)]
     dp_scratch = [take(5) for _ in range(n_dp)]
     rank = lax.axis_index("tensor")
     t_peers = [lax.rem(rank + k, n_t) for k in range(1, n_t)]
@@ -164,20 +307,19 @@
                 for k in order
             }
         )
+    in_line = [
+        triple for triple in zip(gather_in, gather_out, gather_sems) if len(triple[2].shape) == 4
+    ]
     gathers = []
     for src, dst, sems in zip(gather_in, gather_out, gather_sems):
-        rows = src.shape[0]
-        own = pl.ds(pl.multiple_of(rank * rows, rows), rows)
-        for k, peer in enumerate(t_peers):
-            gathers.append(remote(src, dst.at[own], sems, k, "tensor", peer))
-    reduces = []
-    for src, (landed, sems) in zip(reduce_in, reduce_scratch):
-        rows = landed.shape[1]
-        copies = []
-        for k, peer in enumerate(t_peers):
-            part = pl.ds(pl.multiple_of(peer * rows, rows), rows)
-            copies.append(remote(src.at[part], landed.at[k], sems, k, "tensor", peer))
-        reduces.append(copies)
+        if len(sems.shape) == 2:
+            rows = src.shape[0]
+            own = pl.ds(pl.multiple_of(rank * rows, rows), rows)
+            for k, peer in enumerate(t_peers):
+                gathers.append(remote(src, dst.at[own], sems, k, "tensor", peer))
+    reduces = [(src, *scratch) for src, scratch in zip(reduce_in, reduce_scratch)]
+    gather_step(rank, n_t, 0, in_line)
+    reduce_step(rank, n_t, reduces, 0)
     second_phase = []
     for src, out, copies, (near, outgoing, far, near_sems, far_sems) in zip(
         dp_in, dp_out, first_phase, dp_scratch
@@ -199,13 +341,10 @@
     for src, dst in zip(gather_in, gather_out):
         rows = src.shape[0]
         dst[pl.ds(pl.multiple_of(rank * rows, rows), rows), :] = src[...]
-    for src, out, copies, (landed, sems) in zip(reduce_in, reduce_out, reduces, reduce_scratch):
-        rows = landed.shape[1]
-        total = src[pl.ds(pl.multiple_of(rank * rows, rows), rows), :].astype(jnp.float32)
-        for k, copy in enumerate(copies):
-            copy.wait_recv()
-            total = total + landed[k].astype(jnp.float32)
-        out[...] = total
+    reduce_step(rank, n_t, reduces, 1)
+    for distance in range(1, n_t):
+        gather_step(rank, n_t, distance, in_line)
+    reduce_total(rank, n_t, reduces, reduce_out)
     for copy in gathers:
         copy.wait_recv()
     for out, later, scratch in zip(dp_out, second_phase, dp_scratch):
@@ -216,7 +355,9 @@
         out[...] = total
     for copy in gathers:
         copy.wait_send()
-    for copies in reduces + second_phase:
+    gather_finish(rank, n_t, in_line)
+    reduce_step(rank, n_t, reduces, 2)
+    for copies in second_phase:
         for copy in copies:
             copy.wait_send()
     for copies in first_phase:
@@ -233,12 +374,15 @@
     inputs = list(gathers) + list(reduces)
     for value in gathers:
         outs.append(jax.ShapeDtypeStruct((n_t * value.shape[0], value.shape[1]), value.dtype))
-        scratch.append(pltpu.SemaphoreType.DMA((2, n_t - 1)))
+        lined = value.shape[0] % (16 * PIECES) == 0
+        shape = (2, 2, n_t - 1, PIECES) if lined else (2, n_t - 1)
+        scratch.append(pltpu.SemaphoreType.DMA(shape))
     for value in reduces:
         rows, columns = value.shape[0] // n_t, value.shape[1]
         outs.append(jax.ShapeDtypeStruct((rows, columns), jnp.float32))
-        scratch.append(pltpu.VMEM((n_t - 1, rows, columns), value.dtype))
-        scratch.append(pltpu.SemaphoreType.DMA((2, n_t - 1)))
+        scratch.append(pltpu.VMEM((2, n_t - 1, rows, columns), value.dtype))
+        scratch.append(pltpu.VMEM((2, n_t - 1, rows, columns), value.dtype))
+        scratch.append(pltpu.SemaphoreType.DMA((2, 2, n_t - 1, PIECES)))
     n_dp = 0
     if by_kernel:
         for value in dp_reduces:

time: 230 us -> 196 us (0.85)
  Pallas kernels: 167 us -> 133 us
    pallas_call x7, Pallas kernels: 155 us -> 124 us  [exchange(): pl.pallas_call(partial(exchange_kernel, n_t, n_d, len(gathers), len(reduc...]
where the time goes in v2:
time: 196 us
  Pallas kernels  133 us (68%)
  matrix products  26.2 us (13%)
  local copies, waits for them, and re-layouts  19.1 us (10%)
  other arithmetic  15.4 us (8%)
    pallas_call x7, Pallas kernels, exchange(): pl.pallas_call(partial(exchange_kernel, n_t, n_d, len(gathers), len(reduc...  124 us
    unnamed x103, local copies, waits for them, and re-layouts  11.7 us
    dot_general x12, matrix products, left_contract(): lax.dot_general(left, right, (((0,), (0,)), ((), ())), preferred_element_...  9.83 us
    pallas_call x1, Pallas kernels, gather_vectors(): pl.pallas_call(partial(vector_kernel, n_t, n_d), out_shape=[jax.ShapeDtyp...  9.38 us
    dot_general x13, matrix products, matmul(): return jnp.dot(left, right, preferred_element_type=jnp.float32)  8.51 us
    dot_general x12, matrix products, right_contract(): lax.dot_general(left, right, (((1,), (1,)), ((), ())), preferred_element_...  6.44 us

profile of v2, /device:TPU:0, one launch (start us, length us, event | category | flops | bytes accessed | tf_op | source)
XLA Modules:
  0.0 195.6 jit_solution(10090278864094337671)
XLA Ops:
  0.7 1.2 convert_reduce_fusion.3
  1.9 1.1 fusion.40
  3.0 1.3 convert_reduce_fusion.6
  5.1 1.0 convolution_reduce_fusion
  6.2 7.4 %exchange_0.1 = f32[64,128]{1,0:T(8,128)S(1)} custom-call(f32[16,128]{1,0:T(8,128)S(1)} %pad_bitcast_fusion.2.refs_0_), custom_call_target="tpu_custom_call" | custom-call | tf_op jit(solution)/shard_map/exchange_0/pallas_call | solution.py:400
  14.0 28.9 %exchange_1.1 = (bf16[512,768]{1,0:T(8,128)(2,1)S(1)}, bf16[512,768]{1,0:T(8,128)(2,1)S(1)}) custom-call(bf16[128,768]{1,0:T(8,128)(2,1)S(1)} %get-tuple-element.102.refs_0_, bf16[128,768]{1,0:T(8,128)(2,1)S(1)} %get-tuple-element.103.refs_1_), custom_call_target="tpu_custom_call" | custom-call | tf_op jit(solution)/shard_map/exchange_1/pallas_call | solution.py:400
  43.7 1.4 fusion.8
  49.6 17.3 %exchange_2.1 = f32[128,768]{1,0:T(8,128)S(1)} custom-call(bf16[512,768]{1,0:T(8,128)(2,1)S(1)} %convolution_convert_fusion.4.refs_0_), custom_call_target="tpu_custom_call" | custom-call | tf_op jit(solution)/shard_map/exchange_2/pallas_call | solution.py:400
  67.5 14.0 %exchange_3.1 = bf16[512,768]{1,0:T(8,128)(2,1)S(1)} custom-call(bf16[128,768]{1,0:T(8,128)(2,1)S(1)} %add_convert_fusion.2.refs_0_), custom_call_target="tpu_custom_call" | custom-call | tf_op jit(solution)/shard_map/exchange_3/pallas_call | solution.py:400
  82.8 2.3 %convert_reduce_fusion.1 = (f32[768]{0:T(1024)}, bf16[512,768]{1,0:T(8,128)(2,1)S(1)}, f32[512,768]{1,0:T(8,128)S(1)}) fusion(f32[512,768]{1,0:T(8,128)S(1)} %fusion.104, f32[768]{0:T(1024)S(1)} %copy-done.43, bf16[512,768]{1,0:T(8,128)(2,1)S(1)} %exchange_3.1, bf16[768,768]{1,0:T(8,128)(2,1)S(1)} %copy-done.41), kind=kOutput, calls=%fused_computation.10 | convolution fusion | flops 613022976 | bytes 5904384 | tf_op jit(solution)/shard_map/dot_general | solution.py:33
  87.6 1.1 convolution_convert_fusion.2.refs_1_
  88.7 21.5 %exchange_4.1 = (f32[128,768]{1,0:T(8,128)S(1)}, f32[128,768]{1,0:T(8,128)S(1)}) custom-call(bf16[512,768]{1,0:T(8,128)(2,1)S(1)} %convolution_convert_fusion.3.refs_0_, bf16[512,768]{1,0:T(8,128)(2,1)S(1)} %convolution_convert_fusion.2.refs_1_), custom_call_target="tpu_custom_call" | custom-call | tf_op jit(solution)/shard_map/exchange_4/pallas_call | solution.py:400
  111.0 1.7 fusion.42
  113.7 17.4 %exchange_5.1 = (bf16[512,768]{1,0:T(8,128)(2,1)S(1)}, f32[96,768]{1,0:T(8,128)S(1)}, f32[96,768]{1,0:T(8,128)S(1)}) custom-call(bf16[128,768]{1,0:T(8,128)(2,1)S(1)} %multiply_convert_fusion.4.refs_0_, bf16[4,2,96,768]{3,2,1,0:T(8,128)(2,1)S(1)} %bitcast.80, bf16[4,2,96,768]{3,2,1,0:T(8,128)(2,1)S(1)} %bitcast.81), custom_call_target="tpu_custom_call" | custom-call | tf_op jit(solution)/shard_map/exchange_5/pallas_call | solution.py:400
  131.2 1.0 convolution_convert_fusion.5
  134.3 1.0 convolution_convert_fusion.6
  140.9 1.4 concatenate.30
  143.0 1.2 convolution_convert_fusion.7
  144.2 1.2 convolution_convert_fusion.8
  145.4 1.1 pad_maximum_fusion
  146.5 1.6 copy.28
  148.2 1.4 fusion.48
  150.6 17.4 %exchange_6.1 = (f32[128,768]{1,0:T(8,128)S(1)}, f32[96,768]{1,0:T(8,128)S(1)}) custom-call(bf16[512,768]{1,0:T(8,128)(2,1)S(1)} %add_convert_fusion.refs_0_, bf16[4,2,96,768]{3,2,1,0:T(8,128)(2,1)S(1)} %bitcast.79), custom_call_target="tpu_custom_call" | custom-call | tf_op jit(solution)/shard_map/exchange_6/pallas_call | solution.py:400
  169.0 1.3 constant_dynamic-update-slice_fusion.5
  170.3 1.3 constant_dynamic-update-slice_fusion.4
  171.6 1.3 constant_dynamic-update-slice_fusion.3
  172.9 1.3 constant_dynamic-update-slice_fusion.2
  174.2 1.3 constant_dynamic-update-slice_fusion.1
  175.5 1.3 constant_dynamic-update-slice_fusion
  177.5 1.9 fusion.38
  181.4 9.4 %gather_vectors.1 = (f32[8,32,128]{2,1,0:T(8,128)S(1)}, f32[8,16,128]{2,1,0:T(8,128)S(1)}) custom-call(f32[32,128]{1,0:T(8,128)S(1)} %pad_bitcast_fusion.1.first, f32[4,16,128]{2,1,0:T(8,128)S(1)} %bitcast.84), custom_call_target="tpu_custom_call" | custom-call | tf_op jit(solution)/shard_map/gather_vectors/pallas_call | solution.py:458
  192.8 1.4 fusion.84
  (171 shorter events, 28.6 us)
Async XLA Ops:
  0.6 4.5 %copy-start = (bf16[768,1152]{1,0:T(8,128)(2,1)S(1)}, bf16[768,1152]{1,0:T(8,128)(2,1)}, u32[]{:S(2)}) copy-start(bf16[768,1152]{1,0:T(8,128)(2,1)} %param.15) | copy-start | bytes 5308420
  0.7 13.1 %copy-start.7 = (bf16[128,768]{1,0:T(8,128)(2,1)S(1)}, bf16[128,768]{1,0:T(8,128)(2,1)}, u32[]{:S(2)}) copy-start(bf16[128,768]{1,0:T(8,128)(2,1)} %param.13) | copy-start | bytes 589828
  0.7 13.1 %copy-start.10 = (bf16[128,768]{1,0:T(8,128)(2,1)S(1)}, bf16[128,768]{1,0:T(8,128)(2,1)}, u32[]{:S(2)}) copy-start(bf16[128,768]{1,0:T(8,128)(2,1)} %param.25) | copy-start | bytes 589828
  0.7 5.5 %copy-start.36 = (f32[1152]{0:T(1024)S(1)}, f32[1152]{0:T(1024)}, u32[]{:S(2)}) copy-start(f32[1152]{0:T(1024)} %param.16) | copy-start | bytes 13828
  1.9 41.0 %copy-start.34 = (f32[128]{0:T(128)}, f32[128]{0:T(128)S(1)}, u32[]{:S(2)}) copy-start(f32[128]{0:T(128)S(1)} %broadcast_multiply_fusion.5) | copy-start | bytes 1540
  3.0 39.9 %copy-start.38 = (f32[128]{0:T(128)}, f32[128]{0:T(128)S(1)}, u32[]{:S(2)}) copy-start(f32[128]{0:T(128)S(1)} %add_rsqrt_fusion.1) | copy-start | bytes 1540
  13.7 31.3 %copy-start.26 = (f32[768]{0:T(1024)}, f32[768]{0:T(1024)S(1)}, u32[]{:S(2)}) copy-start(f32[768]{0:T(1024)S(1)} %get-tuple-element.70) | copy-start | bytes 9220
  13.8 31.3 %copy-start.8 = (bf16[3,768,192]{1,2,0:T(8,128)(2,1)S(1)}, bf16[3,768,192]{1,2,0:T(8,128)(2,1)}, u32[]{:S(2)}) copy-start(bf16[3,768,192]{1,2,0:T(8,128)(2,1)} %param.17) | copy-start | bytes 2654212
  49.2 17.7 %copy-start.28 = (f32[768]{0:T(1024)S(1)}, f32[768]{0:T(1024)}, u32[]{:S(2)}) copy-start(f32[768]{0:T(1024)} %param.20) | copy-start | bytes 9220
  66.9 14.6 %copy-start.42 = (bf16[768,768]{1,0:T(8,128)(2,1)S(1)}, bf16[768,768]{1,0:T(8,128)(2,1)}, u32[]{:S(2)}) copy-start(bf16[768,768]{1,0:T(8,128)(2,1)} %param.23) | copy-start | bytes 3538948
  88.7 22.3 %copy-start.40 = (f32[768]{0:T(1024)S(1)}, f32[768]{0:T(1024)}, u32[]{:S(2)}) copy-start(f32[768]{0:T(1024)} %param.24) | copy-start | bytes 9220
  133.3 2.4 %copy-start.11 = (bf16[512,64]{0,1:T(8,128)(2,1)}, bf16[512,64]{0,1:T(8,128)(2,1)S(1)}, u32[]{:S(2)}) copy-start(bf16[512,64]{0,1:T(8,128)(2,1)S(1)} %convolution_convert_fusion.15) | copy-start | bytes 196612
  133.6 2.1 %copy-start.13 = (bf16[512,64]{0,1:T(8,128)(2,1)}, bf16[512,64]{0,1:T(8,128)(2,1)S(1)}, u32[]{:S(2)}) copy-start(bf16[512,64]{0,1:T(8,128)(2,1)S(1)} %convolution_convert_fusion.14) | copy-start | bytes 196612
  136.2 4.5 %copy-start.15 = (bf16[512,64]{0,1:T(8,128)(2,1)}, bf16[512,64]{0,1:T(8,128)(2,1)S(1)}, u32[]{:S(2)}) copy-start(bf16[512,64]{0,1:T(8,128)(2,1)S(1)} %fusion.14) | copy-start | bytes 196612
  138.0 2.7 %copy-start.17 = (bf16[512,64]{0,1:T(8,128)(2,1)}, bf16[512,64]{0,1:T(8,128)(2,1)S(1)}, u32[]{:S(2)}) copy-start(bf16[512,64]{0,1:T(8,128)(2,1)S(1)} %fusion.13) | copy-start | bytes 196612
  139.3 3.7 %copy-start.22 = (bf16[512,64]{0,1:T(8,128)(2,1)S(1)}, bf16[512,64]{0,1:T(8,128)(2,1)}, u32[]{:S(2)}) copy-start(bf16[512,64]{0,1:T(8,128)(2,1)} %fusion.11) | copy-start | bytes 196612
  140.7 4.7 %copy-start.19 = (bf16[768,192]{0,1:T(8,128)(2,1)S(1)}, bf16[768,192]{0,1:T(8,128)(2,1)}, u32[]{:S(2)}) copy-start(bf16[768,192]{0,1:T(8,128)(2,1)} %convolution_convert_fusion.5) | copy-start | bytes 884740
  140.7 4.7 %copy-start.20 = (bf16[768,192]{0,1:T(8,128)(2,1)S(1)}, bf16[768,192]{0,1:T(8,128)(2,1)}, u32[]{:S(2)}) copy-start(bf16[768,192]{0,1:T(8,128)(2,1)} %convolution_convert_fusion.6) | copy-start | bytes 884740
  146.5 1.7 copy-start.16
  146.5 1.7 copy-start.18
  148.2 1.9 copy-start.12
  148.2 1.9 copy-start.14
  150.5 18.2 %copy-start.27 = (f32[768]{0:T(1024)S(1)}, f32[768]{0:T(1024)}, u32[]{:S(2)}) copy-start(f32[768]{0:T(1024)} %copy-done.26) | copy-start | bytes 9220
  150.5 18.2 %copy-start.35 = (f32[128]{0:T(128)S(1)}, f32[128]{0:T(128)}, u32[]{:S(2)}) copy-start(f32[128]{0:T(128)} %copy-done.34) | copy-start | bytes 1540
  150.6 18.2 %copy-start.39 = (f32[128]{0:T(128)S(1)}, f32[128]{0:T(128)}, u32[]{:S(2)}) copy-start(f32[128]{0:T(128)} %copy-done.38) | copy-start | bytes 1540
  150.6 21.0 %copy-start.32 = (f32[768]{0:T(1024)S(1)}, f32[768]{0:T(1024)}, u32[]{:S(2)}) copy-start(f32[768]{0:T(1024)} %get-tuple-element.80) | copy-start | bytes 9220
  150.6 22.3 %copy-start.30 = (f32[768]{0:T(1024)S(1)}, f32[768]{0:T(1024)}, u32[]{:S(2)}) copy-start(f32[768]{0:T(1024)} %get-tuple-element.64) | copy-start | bytes 9220
  150.6 23.6 %copy-start.29 = (f32[768]{0:T(1024)S(1)}, f32[768]{0:T(1024)}, u32[]{:S(2)}) copy-start(f32[768]{0:T(1024)} %get-tuple-element.58) | copy-start | bytes 9220
  150.6 24.9 %copy-start.31 = (f32[768]{0:T(1024)S(1)}, f32[768]{0:T(1024)}, u32[]{:S(2)}) copy-start(f32[768]{0:T(1024)} %get-tuple-element.78) | copy-start | bytes 9220
  168.7 10.7 %copy-start.2 = (f32[96,768]{1,0:T(8,128)S(1)}, f32[96,768]{1,0:T(8,128)}, u32[]{:S(2)}) copy-start(f32[96,768]{1,0:T(8,128)} %copy-done.1) | copy-start | bytes 884740
  179.5 14.7 %copy-start.6 = (f32[96,768]{1,0:T(8,128)S(1)}, f32[96,768]{1,0:T(8,128)}, u32[]{:S(2)}) copy-start(f32[96,768]{1,0:T(8,128)} %copy-done.5) | copy-start | bytes 884740
  179.6 15.3 %copy-start.4 = (f32[96,768]{1,0:T(8,128)S(1)}, f32[96,768]{1,0:T(8,128)}, u32[]{:S(2)}) copy-start(f32[96,768]{1,0:T(8,128)} %copy-done.3) | copy-start | bytes 884740
  (12 other events, 16.8 us)

commit v3 on v2

--- a/solution.py
+++ b/solution.py
@@ -414,19 +414,38 @@
     return results
 
 
-def vector_kernel(n_t, n_d, first, shares, first_all, share_all, landed, total, *sems):
+def row_terms(grade_a, normed_a, mid, branch_a, grade_f, normed_f, tangent, branch_f):
+    return (
+        grade_a,
+        grade_a * normed_a,
+        mid * branch_a,
+        grade_f,
+        grade_f * normed_f,
+        tangent * branch_f,
+    )
+
+
+def vector_kernel(n_t, n_d, lanes, first, *refs):
+    rows, (first_all, share_all, shares, landed, total, *sems) = refs[:8], refs[8:]
     first_sems, part_sems, total_sems = sems
     rank, place = lax.axis_index("tensor"), lax.axis_index("dp")
     t_peers = [lax.rem(rank + k, n_t) for k in range(1, n_t)]
     d_peers = [lax.rem(place + k, n_d) for k in range(1, n_d)]
     greet([("tensor", t_peers), ("dp", d_peers)])
+    copies = [
+        remote(first, first_all.at[place], first_sems, k, "dp", peer)
+        for k, peer in enumerate(d_peers)
+    ]
+    shares[...] = jnp.zeros_like(shares)
+    for member, term in enumerate(row_terms(*[ref[...].astype(jnp.float32) for ref in rows])):
+        line = jnp.sum(term, axis=0, keepdims=True)
+        per_member = line.shape[1] // 128
+        for i in range(per_member):
+            owner, row = divmod(member * per_member + i, lanes)
+            shares[owner, row : row + 1, :] = line[:, i * 128 : (i + 1) * 128]
     parts = [
         remote(shares.at[peer], landed.at[k], part_sems, k, "tensor", peer)
         for k, peer in enumerate(t_peers)
-    ]
-    copies = [
-        remote(first, first_all.at[place], first_sems, k, "dp", peer)
-        for k, peer in enumerate(d_peers)
     ]
     value = shares[rank]
     for k, copy in enumerate(parts):
@@ -445,25 +464,26 @@
         copy.wait_send()
 
 
-def gather_vectors(ident, first, shares):
+def gather_vectors(ident, first, rows):
     n_t, n_d = lax.axis_size("tensor"), lax.axis_size("dp")
-    if n_d > 8:
+    if n_d > 8 or rows[0].shape[1] % 128 or 6 * rows[0].shape[1] % (n_t * 128):
+        terms = row_terms(*[value.astype(jnp.float32) for value in rows])
+        shares = jnp.concatenate([jnp.sum(term, axis=0) for term in terms])
         total = lax.psum_scatter(shares, "tensor", scatter_dimension=0, tiled=True)
         return (lax.all_gather(first, "dp"), lax.all_gather(total, "dp"))
-    length, width = first.shape[0], shares.shape[0] // n_t
+    length, width = first.shape[0], 6 * rows[0].shape[1] // n_t
     length_rows, width_rows = -(-length // 1024) * 8, -(-width // 1024) * 8
     first = jnp.pad(first, (0, length_rows * 128 - length)).reshape(length_rows, 128)
-    shares = jnp.pad(shares.reshape(n_t, width), ((0, 0), (0, width_rows * 128 - width)))
-    shares = shares.reshape(n_t, width_rows, 128)
     first_all, share_all = pl.pallas_call(
-        partial(vector_kernel, n_t, n_d),
+        partial(vector_kernel, n_t, n_d, width // 128),
         out_shape=[
             jax.ShapeDtypeStruct((n_d, length_rows, 128), jnp.float32),
             jax.ShapeDtypeStruct((n_d, width_rows, 128), jnp.float32),
         ],
-        in_specs=[pl.BlockSpec(memory_space=pltpu.VMEM)] * 2,
+        in_specs=[pl.BlockSpec(memory_space=pltpu.VMEM)] * 9,
         out_specs=[pl.BlockSpec(memory_space=pltpu.VMEM)] * 2,
         scratch_shapes=[
+            pltpu.VMEM((n_t, width_rows, 128), jnp.float32),
             pltpu.VMEM((n_t - 1, width_rows, 128), jnp.float32),
             pltpu.VMEM((width_rows, 128), jnp.float32),
             pltpu.SemaphoreType.DMA((2, n_d - 1)),
@@ -472,7 +492,7 @@
         ],
         compiler_params=pltpu.CompilerParams(collective_id=ident, **PARAMS),
         name="gather_vectors",
-    )(first, shares)
+    )(first, *rows)
     return (
         first_all.reshape(n_d, -1)[:, :length],
         share_all.reshape(n_d, -1)[:, :width],
@@ -564,23 +584,20 @@
     token_grad = mid_grad + norm_back(
         attn_in_grad * (1.0 + scale_attn), normed_first, inverse_first
     )
-    modulation_partial = jnp.concatenate(
-        [
-            jnp.sum(term, axis=0)
-            for term in (
-                attn_in_grad,
-                attn_in_grad * normed_first,
-                mid_grad * branch_attn,
-                feed_in_grad,
-                feed_in_grad * normed_second,
-                tangent * branch_feed,
-            )
-        ]
+    rows = (
+        attn_in_grad,
+        normed_first,
+        mid_grad,
+        branch_attn,
+        feed_in_grad,
+        normed_second,
+        cotangent,
+        branch_feed,
     )
     columns = [heads_grad[0], heads_grad[2], attn_grad_all, pre_grad, feed_grad_all]
     sums = [jnp.sum(value, axis=0, dtype=jnp.float32) for value in columns]
     vectors, modulation_all = gather_vectors(
-        7, jnp.concatenate(sums + [silu_cond[0].astype(jnp.float32)]), modulation_partial
+        7, jnp.concatenate(sums + [silu_cond[0].astype(jnp.float32)]), rows
     )
     bias_total = jnp.sum(vectors, axis=0)
     offsets = [0]

time: 196 us -> 194 us (0.990)
  local copies, waits for them, and re-layouts: 19.1 us -> 16.9 us
    unnamed x103 -> x82, local copies, waits for them, and re-layouts: 11.7 us -> 7.68 us
    slice x2, local copies, waits for them, and re-layouts: 0.17 us -> 2.52 us  [local(): inner_share[:, :3 * local_width].reshape(share, 3, local_width)]
    reduce_sum x3 -> x2, other arithmetic: 2.67 us -> 0.35 us  [norm_back(): jnp.mean(grade, axis=-1, keepdims=True)]
    convert_element_type x1, other arithmetic: 0.19 us -> 2.16 us  [local(): output = (residual_mid + gate_feed * branch_feed).astype(low)]
where the time goes in v3:
time: 194 us; the launch traced here: 193 us
  Pallas kernels  133 us (69%)
  matrix products  27 us (14%)
  local copies, waits for them, and re-layouts  16.9 us (9%)
  other arithmetic  14.3 us (7%)
    pallas_call x7, Pallas kernels, exchange(): pl.pallas_call(partial(exchange_kernel, n_t, n_d, len(gathers), len(reduc...  124 us
    dot_general x12, matrix products, left_contract(): lax.dot_general(left, right, (((0,), (0,)), ((), ())), preferred_element_...  10.5 us
    pallas_call x1, Pallas kernels, gather_vectors(): pl.pallas_call(partial(vector_kernel, n_t, n_d, width // 128), out_shape=...  9.67 us
    dot_general x13, matrix products, matmul(): return jnp.dot(left, right, preferred_element_type=jnp.float32)  8.65 us
    unnamed x82, local copies, waits for them, and re-layouts  7.68 us
    dot_general x12, matrix products, right_contract(): lax.dot_general(left, right, (((1,), (1,)), ((), ())), preferred_element_...  6.46 us

profile of v3, /device:TPU:0, one launch (start us, length us, event | category | flops | bytes accessed | tf_op | source)
XLA Modules:
  0.0 193.1 jit_solution(8856372042512813468)
XLA Ops:
  0.7 1.2 convert_reduce_fusion.3
  1.9 1.1 fusion.29
  3.0 1.3 convert_reduce_fusion.6
  5.1 1.0 convolution_reduce_fusion
  6.2 7.4 %exchange_0.1 = f32[64,128]{1,0:T(8,128)S(1)} custom-call(f32[16,128]{1,0:T(8,128)S(1)} %pad_bitcast_fusion.1.refs_0_), custom_call_target="tpu_custom_call" | custom-call | tf_op jit(solution)/shard_map/exchange_0/pallas_call | solution.py:400
  13.8 0.9 fusion.27
  14.7 28.9 %exchange_1.1 = (bf16[512,768]{1,0:T(8,128)(2,1)S(1)}, bf16[512,768]{1,0:T(8,128)(2,1)S(1)}) custom-call(bf16[128,768]{1,0:T(8,128)(2,1)S(1)} %get-tuple-element.79.refs_0_, bf16[128,768]{1,0:T(8,128)(2,1)S(1)} %get-tuple-element.101.refs_1_), custom_call_target="tpu_custom_call" | custom-call | tf_op jit(solution)/shard_map/exchange_1/pallas_call | solution.py:400
  43.8 1.5 fusion.8
  49.8 17.3 %exchange_2.1 = f32[128,768]{1,0:T(8,128)S(1)} custom-call(bf16[512,768]{1,0:T(8,128)(2,1)S(1)} %convolution_convert_fusion.4.refs_0_), custom_call_target="tpu_custom_call" | custom-call | tf_op jit(solution)/shard_map/exchange_2/pallas_call | solution.py:400
  67.7 14.0 %exchange_3.1 = bf16[512,768]{1,0:T(8,128)(2,1)S(1)} custom-call(bf16[128,768]{1,0:T(8,128)(2,1)S(1)} %get-tuple-element.74.refs_0_), custom_call_target="tpu_custom_call" | custom-call | tf_op jit(solution)/shard_map/exchange_3/pallas_call | solution.py:400
  83.0 2.3 %convert_reduce_fusion.1 = (f32[768]{0:T(1024)}, bf16[512,768]{1,0:T(8,128)(2,1)S(1)}, f32[512,768]{1,0:T(8,128)S(1)}) fusion(f32[512,768]{1,0:T(8,128)S(1)} %fusion.92, f32[768]{0:T(1024)S(1)} %copy-done.36, bf16[512,768]{1,0:T(8,128)(2,1)S(1)} %exchange_3.1, bf16[768,768]{1,0:T(8,128)(2,1)S(1)} %copy-done.34), kind=kOutput, calls=%fused_computation.10 | convolution fusion | flops 613022976 | bytes 5904384 | tf_op jit(solution)/shard_map/dot_general | solution.py:33
  87.0 0.9 convolution_convert_fusion
  87.9 1.1 convolution_convert_fusion.2.refs_1_
  89.0 21.6 %exchange_4.1 = (f32[128,768]{1,0:T(8,128)S(1)}, f32[128,768]{1,0:T(8,128)S(1)}) custom-call(bf16[512,768]{1,0:T(8,128)(2,1)S(1)} %convolution_convert_fusion.3.refs_0_, bf16[512,768]{1,0:T(8,128)(2,1)S(1)} %convolution_convert_fusion.2.refs_1_), custom_call_target="tpu_custom_call" | custom-call | tf_op jit(solution)/shard_map/exchange_4/pallas_call | solution.py:400
  111.5 17.3 %exchange_5.1 = (bf16[512,768]{1,0:T(8,128)(2,1)S(1)}, f32[96,768]{1,0:T(8,128)S(1)}, f32[96,768]{1,0:T(8,128)S(1)}) custom-call(bf16[128,768]{1,0:T(8,128)(2,1)S(1)} %get-tuple-element.70.refs_0_, bf16[4,2,96,768]{3,2,1,0:T(8,128)(2,1)S(1)} %bitcast.75, bf16[4,2,96,768]{3,2,1,0:T(8,128)(2,1)S(1)} %bitcast.76), custom_call_target="tpu_custom_call" | custom-call | tf_op jit(solution)/shard_map/exchange_5/pallas_call | solution.py:400
  129.6 1.0 convolution_convert_fusion.5
  132.7 1.0 convolution_convert_fusion.6
  136.3 0.9 fusion.10
  138.1 0.9 fusion.9
  139.2 1.4 concatenate.27
  141.3 1.6 convolution_convert_fusion.7
  142.9 1.5 convolution_convert_fusion.8
  144.4 1.1 pad_maximum_fusion
  145.5 2.4 %copy.28 = bf16[768,768]{1,0:T(8,128)(2,1)} copy(bf16[768,768]{0,1:T(8,128)(2,1)} %pad_maximum_fusion) | data formatting | bytes 2359296 | tf_op jit(solution)/shard_map/concatenate | solution.py:576
  147.9 1.5 fusion.36
  151.1 17.3 %exchange_6.1 = (f32[128,768]{1,0:T(8,128)S(1)}, f32[96,768]{1,0:T(8,128)S(1)}) custom-call(bf16[512,768]{1,0:T(8,128)(2,1)S(1)} %add_convert_fusion.refs_0_, bf16[4,2,96,768]{3,2,1,0:T(8,128)(2,1)S(1)} %bitcast.74), custom_call_target="tpu_custom_call" | custom-call | tf_op jit(solution)/shard_map/exchange_6/pallas_call | solution.py:400
  171.1 1.6 copy.31
  172.8 1.8 copy.29
  174.6 1.8 copy.30
  176.4 2.2 %add_convert_fusion.1 = (bf16[128,768]{1,0:T(8,128)(2,1)}, f32[128,768]{1,0:T(8,128)S(1)}, f32[128,768]{1,0:T(8,128)}) fusion(f32[768]{0:T(1024)} %copy-done.25, f32[128,768]{1,0:T(8,128)S(1)} %get-tuple-element.77.refs_3_, f32[768]{0:T(1024)} %copy-done.22, bf16[128,768]{1,0:T(8,128)(2,1)} %param.13, f32[128,768]{1,0:T(8,128)} %copy-done.6, f32[768]{0:T(1024)} %param.24, ...), kind=kLoop, calls=%fused_computation.92 | loop fusion | flops 1474560 | bytes 2766848 | tf_op jit(solution)/shard_map/convert_element_type | solution.py:562
  178.6 9.7 %gather_vectors.1 = (f32[8,32,128]{2,1,0:T(8,128)S(1)}, f32[8,16,128]{2,1,0:T(8,128)S(1)}) custom-call(f32[32,128]{1,0:T(8,128)S(1)} %pad_bitcast_fusion.first, f32[128,768]{1,0:T(8,128)S(1)} %get-tuple-element.28.refs_0_, f32[128,768]{1,0:T(8,128)S(1)} %copy-done.5, f32[128,768]{1,0:T(8,128)S(1)} %get-tuple-element.71.refs_2_, ...), custom_call_target="tpu_custom_call" | custom-call | tf_op jit(solution)/shard_map/gather_vectors/pallas_call | solution.py:477
  190.3 1.4 fusion.72
  (146 shorter events, 24.8 us)
Async XLA Ops:
  0.6 4.5 %copy-start = (bf16[768,1152]{1,0:T(8,128)(2,1)S(1)}, bf16[768,1152]{1,0:T(8,128)(2,1)}, u32[]{:S(2)}) copy-start(bf16[768,1152]{1,0:T(8,128)(2,1)} %param.15) | copy-start | bytes 5308420
  0.7 13.1 %copy-start.12 = (bf16[128,768]{1,0:T(8,128)(2,1)S(1)}, bf16[128,768]{1,0:T(8,128)(2,1)}, u32[]{:S(2)}) copy-start(bf16[128,768]{1,0:T(8,128)(2,1)} %param.13) | copy-start | bytes 589828
  0.7 13.1 %copy-start.4 = (bf16[128,768]{1,0:T(8,128)(2,1)S(1)}, bf16[128,768]{1,0:T(8,128)(2,1)}, u32[]{:S(2)}) copy-start(bf16[128,768]{1,0:T(8,128)(2,1)} %refs_6_.1) | copy-start | bytes 589828
  0.7 5.5 %copy-start.29 = (f32[1152]{0:T(1024)S(1)}, f32[1152]{0:T(1024)}, u32[]{:S(2)}) copy-start(f32[1152]{0:T(1024)} %param.16) | copy-start | bytes 13828
  1.9 12.8 %copy-start.27 = (f32[128]{0:T(128)}, f32[128]{0:T(128)S(1)}, u32[]{:S(2)}) copy-start(f32[128]{0:T(128)S(1)} %broadcast_multiply_fusion.5) | copy-start | bytes 1540
  3.0 11.7 %copy-start.31 = (f32[128]{0:T(128)}, f32[128]{0:T(128)S(1)}, u32[]{:S(2)}) copy-start(f32[128]{0:T(128)S(1)} %add_rsqrt_fusion.1) | copy-start | bytes 1540
  13.7 31.5 %copy-start.23 = (f32[768]{0:T(1024)}, f32[768]{0:T(1024)S(1)}, u32[]{:S(2)}) copy-start(f32[768]{0:T(1024)S(1)} %get-tuple-element.66) | copy-start | bytes 9220
  13.7 31.5 %copy-start.25 = (f32[768]{0:T(1024)}, f32[768]{0:T(1024)S(1)}, u32[]{:S(2)}) copy-start(f32[768]{0:T(1024)S(1)} %get-tuple-element.64) | copy-start | bytes 9220
  13.8 97.0 %copy-start.22 = (f32[768]{0:T(1024)}, f32[768]{0:T(1024)S(1)}, u32[]{:S(2)}) copy-start(f32[768]{0:T(1024)S(1)} %get-tuple-element.67) | copy-start | bytes 9220
  14.7 30.6 %copy-start.14 = (bf16[3,768,192]{1,2,0:T(8,128)(2,1)S(1)}, bf16[3,768,192]{1,2,0:T(8,128)(2,1)}, u32[]{:S(2)}) copy-start(bf16[3,768,192]{1,2,0:T(8,128)(2,1)} %param.17) | copy-start | bytes 2654212
  43.6 89.1 %copy-start.11 = (bf16[512,768]{1,0:T(8,128)(2,1)}, bf16[512,768]{1,0:T(8,128)(2,1)S(1)}, u32[]{:S(2)}) copy-start(bf16[512,768]{1,0:T(8,128)(2,1)S(1)} %get-tuple-element.23) | copy-start | bytes 2359300
  49.4 17.7 %copy-start.33 = (f32[768]{0:T(1024)S(1)}, f32[768]{0:T(1024)}, u32[]{:S(2)}) copy-start(f32[768]{0:T(1024)} %param.20) | copy-start | bytes 9220
  67.3 14.4 %copy-start.35 = (bf16[768,768]{1,0:T(8,128)(2,1)S(1)}, bf16[768,768]{1,0:T(8,128)(2,1)}, u32[]{:S(2)}) copy-start(bf16[768,768]{1,0:T(8,128)(2,1)} %param.23) | copy-start | bytes 3538948
  81.8 1.3 copy-start.34
  128.8 2.3 %copy-start.7 = (f32[96,768]{1,0:T(8,128)}, f32[96,768]{1,0:T(8,128)S(1)}, u32[]{:S(2)}) copy-start(f32[96,768]{1,0:T(8,128)S(1)} %get-tuple-element.33) | copy-start | bytes 884740
  128.8 2.3 %copy-start.9 = (f32[96,768]{1,0:T(8,128)}, f32[96,768]{1,0:T(8,128)S(1)}, u32[]{:S(2)}) copy-start(f32[96,768]{1,0:T(8,128)S(1)} %get-tuple-element.122) | copy-start | bytes 884740
  137.6 1.5 copy-start.26
  137.6 1.5 copy-start.30
  140.5 3.8 %copy-start.16 = (bf16[768,192]{0,1:T(8,128)(2,1)S(1)}, bf16[768,192]{0,1:T(8,128)(2,1)}, u32[]{:S(2)}) copy-start(bf16[768,192]{0,1:T(8,128)(2,1)} %convolution_convert_fusion.5) | copy-start | bytes 884740
  140.5 3.8 %copy-start.17 = (bf16[768,192]{0,1:T(8,128)(2,1)S(1)}, bf16[768,192]{0,1:T(8,128)(2,1)}, u32[]{:S(2)}) copy-start(bf16[768,192]{0,1:T(8,128)(2,1)} %convolution_convert_fusion.6) | copy-start | bytes 884740
  147.9 1.5 copy-start.15
  147.9 1.5 copy-start.19
  147.9 1.5 copy-start.20
  147.9 1.5 copy-start.21
  151.1 17.3 %copy-start.13 = (bf16[128,768]{1,0:T(8,128)(2,1)S(1)}, bf16[128,768]{1,0:T(8,128)(2,1)}, u32[]{:S(2)}) copy-start(bf16[128,768]{1,0:T(8,128)(2,1)} %param.13) | copy-start | bytes 589828
  151.1 17.4 %copy-start.24 = (f32[768]{0:T(1024)S(1)}, f32[768]{0:T(1024)}, u32[]{:S(2)}) copy-start(f32[768]{0:T(1024)} %copy-done.23) | copy-start | bytes 9220
  151.1 17.4 %copy-start.28 = (f32[128]{0:T(128)S(1)}, f32[128]{0:T(128)}, u32[]{:S(2)}) copy-start(f32[128]{0:T(128)} %copy-done.27) | copy-start | bytes 1540
  151.1 17.4 %copy-start.32 = (f32[128]{0:T(128)S(1)}, f32[128]{0:T(128)}, u32[]{:S(2)}) copy-start(f32[128]{0:T(128)} %copy-done.31) | copy-start | bytes 1540
  176.4 2.2 %copy-start.3 = (f32[128,768]{1,0:T(8,128)S(1)}, f32[128,768]{1,0:T(8,128)}, u32[]{:S(2)}) copy-start(f32[128,768]{1,0:T(8,128)} %copy-done.2) | copy-start | bytes 1179652
  176.4 2.2 %copy-start.5 = (f32[128,768]{1,0:T(8,128)S(1)}, f32[128,768]{1,0:T(8,128)}, u32[]{:S(2)}) copy-start(f32[128,768]{1,0:T(8,128)} %get-tuple-element.78.refs_1_) | copy-start | bytes 1179652
  178.6 13.1 %copy-start.10 = (f32[96,768]{1,0:T(8,128)S(1)}, f32[96,768]{1,0:T(8,128)}, u32[]{:S(2)}) copy-start(f32[96,768]{1,0:T(8,128)} %copy-done.9) | copy-start | bytes 884740
  188.3 4.2 %copy-start.8 = (f32[96,768]{1,0:T(8,128)S(1)}, f32[96,768]{1,0:T(8,128)}, u32[]{:S(2)}) copy-start(f32[96,768]{1,0:T(8,128)} %copy-done.7) | copy-start | bytes 884740
  (5 other events, 5.2 us)
